TPU v7x, 32 devices: a whole 2x2x4 slice. The times are simulated.
32 devices in a mesh: dp: 2 (over x), expert: 16 (over z, y, core).
Axes of the slice: x: 2, y: 2, z: 4, core: 2. Of those that a mesh axis runs over, the one named last changes fastest.
Arguments:
- grad_out: bfloat16 [512, 2048], P(('dp', 'expert')), may hold values from -4 to 4
- x_codes: bfloat16 [512, 2048], P(('dp', 'expert')), may hold values from -6 to 6
- x_scales: bfloat16 [512, 16], P(('dp', 'expert')), may hold values from 0.25 to 4
- combine: bfloat16 [512, 8], P(('dp', 'expert')), may hold values from 0.049804688 to 1
- expert_ids: int32 [512, 8], P(('dp', 'expert')), may hold values from 0 to 15, all different within a row; in each aligned block of 16 rows (0 to 15, 16 to 31, ...) at most 16 rows name the same one
- w_gate: bfloat16 [16, 768, 2048], P('expert', 'dp'), may hold values from -0.125 to 0.125
- w_up: bfloat16 [16, 768, 2048], P('expert', 'dp'), may hold values from -0.125 to 0.125
- w_down: bfloat16 [16, 768, 2048], P('expert', 'dp'), may hold values from -0.21875 to 0.21875
Outputs:
- grad_in: bfloat16 [512, 2048], P(('dp', 'expert'))
- grad_combine: float32 [512, 8], P(('dp', 'expert'))
- grad_gate: bfloat16 [16, 768, 2048], P('expert', 'dp')
- grad_up: bfloat16 [16, 768, 2048], P('expert', 'dp')
- grad_down: bfloat16 [16, 768, 2048], P('expert', 'dp')
Inputs may be any that keep to these rules, and one draw needn't show every extreme that they name: `expert_ids`: each token names 8 different experts. Among the 16 tokens of one device no expert is named more than 16 times, and on some devices some expert is named exactly 16 times.
All inputs are finite; a program needn't handle non-finite values.
Results may differ from a plain program's by a relative error of at most 0.015.
Values may be sent and summed in bfloat16 or wider, within the bound.
A program may use at most 128 MiB of HBM per device.

v0:
```python
import jax
import jax.numpy as jnp
from jax import lax
from jax.sharding import PartitionSpec as P

BLOCK = 128


def slot_table(flat_ids, experts, capacity):
    onehot = (flat_ids[:, None] == jnp.arange(experts, dtype=jnp.int32)[None, :]).astype(jnp.int32)
    before = jnp.cumsum(onehot, axis=0) - onehot
    position = jnp.sum(before * onehot, axis=1)
    slot_index = flat_ids * capacity + position
    return jnp.arange(experts * capacity, dtype=jnp.int32)[:, None] == slot_index[None, :]


def token_owner(placed, tokens, picks):
    return jnp.sum(placed.reshape(placed.shape[0], tokens, picks).astype(jnp.int32), axis=2)


def build_rows(grad_out, x_codes, x_scales, combine, expert_ids, experts, capacity):
    tokens, picks = expert_ids.shape
    placed = slot_table(expert_ids.reshape(-1), experts, capacity)
    owner = token_owner(placed, tokens, picks).astype(jnp.bfloat16)
    grad_rows = jnp.dot(owner, grad_out, preferred_element_type=jnp.float32).astype(jnp.bfloat16)
    code_rows = jnp.dot(owner, x_codes, preferred_element_type=jnp.float32).astype(jnp.bfloat16)
    scale_rows = jnp.dot(owner, x_scales, preferred_element_type=jnp.float32).astype(jnp.bfloat16)
    weight_rows = jnp.dot(
        placed.astype(jnp.bfloat16), combine.reshape(-1), preferred_element_type=jnp.float32
    ).astype(jnp.bfloat16)
    return (
        grad_rows.reshape(experts, capacity, -1),
        code_rows.reshape(experts, capacity, -1),
        scale_rows.reshape(experts, capacity, -1),
        weight_rows.reshape(experts, capacity),
    )


def body(grad_out, x_codes, x_scales, combine, expert_ids, w_gate, w_up, w_down):
    tokens, picks = expert_ids.shape
    width = grad_out.shape[1]
    groups = lax.axis_size("dp")
    experts = w_gate.shape[0] * lax.axis_size("expert")
    capacity = min(tokens, max(2, 2 * tokens * picks // experts))
    grad_rows, code_rows, scale_rows, weight_rows = build_rows(
        grad_out, x_codes, x_scales, combine, expert_ids, experts, capacity
    )
    grad_rows, code_rows, scale_rows, weight_rows = (
        lax.all_to_all(grad_rows, "expert", split_axis=0, concat_axis=0, tiled=True),
        lax.all_to_all(code_rows, "expert", split_axis=0, concat_axis=0, tiled=True),
        lax.all_to_all(scale_rows, "expert", split_axis=0, concat_axis=0, tiled=True),
        lax.all_to_all(weight_rows, "expert", split_axis=0, concat_axis=0, tiled=True),
    )
    grad_rows, code_rows, scale_rows, weight_rows = (
        lax.all_gather(grad_rows[None], "dp", axis=0, tiled=True),
        lax.all_gather(code_rows[None], "dp", axis=0, tiled=True),
        lax.all_gather(scale_rows[None], "dp", axis=0, tiled=True),
        lax.all_gather(weight_rows[None], "dp", axis=0, tiled=True),
    )
    rows = groups * experts * capacity
    scale_count = width // BLOCK
    grad_flat = grad_rows.reshape(rows, width)
    x_rows = (
        (
            code_rows.reshape(rows, scale_count, BLOCK).astype(jnp.float32)
            * scale_rows.reshape(rows, scale_count, 1).astype(jnp.float32)
        )
        .reshape(rows, width)
        .astype(jnp.bfloat16)
    )
    weight_flat = weight_rows.reshape(rows).astype(jnp.float32)
    share = w_gate.shape[1]
    stacked_w = jnp.concatenate([w_gate[0], w_up[0]], axis=0)
    down_w = w_down[0]
    both_pre = lax.dot_general(
        x_rows, stacked_w, (((1,), (1,)), ((), ())), preferred_element_type=jnp.float32
    )
    gate_pre = both_pre[:, :share]
    up_pre = both_pre[:, share:]
    sigmoid_gate = jax.nn.sigmoid(gate_pre)
    activated = gate_pre * sigmoid_gate
    hidden = (activated * up_pre).astype(jnp.bfloat16)
    scaled = (weight_flat[:, None] * grad_flat.astype(jnp.float32)).astype(jnp.bfloat16)
    backward = lax.dot_general(
        grad_flat, down_w, (((1,), (1,)), ((), ())), preferred_element_type=jnp.float32
    )
    partial_comb = jnp.sum(backward * hidden.astype(jnp.float32), axis=1)
    grad_hidden = weight_flat[:, None] * backward
    grad_gate_pre = (
        grad_hidden * up_pre * sigmoid_gate * (1.0 + gate_pre * (1.0 - sigmoid_gate))
    ).astype(jnp.bfloat16)
    grad_up_pre = (grad_hidden * activated).astype(jnp.bfloat16)
    grad_both_pre = jnp.concatenate([grad_gate_pre, grad_up_pre], axis=1)
    grad_down = lax.dot_general(
        hidden, scaled, (((0,), (0,)), ((), ())), preferred_element_type=jnp.float32
    ).astype(jnp.bfloat16)
    grad_stacked = lax.dot_general(
        grad_both_pre, x_rows, (((0,), (0,)), ((), ())), preferred_element_type=jnp.float32
    ).astype(jnp.bfloat16)
    grad_gate = grad_stacked[:share]
    grad_up = grad_stacked[share:]
    input_part = jnp.dot(grad_both_pre, stacked_w, preferred_element_type=jnp.float32)
    summed = lax.psum_scatter(
        input_part.reshape(groups, experts, capacity, width).astype(jnp.bfloat16),
        "dp",
        scatter_dimension=0,
        tiled=True,
    ).astype(jnp.float32)
    comb_all = lax.psum(partial_comb, "dp")
    own_terms = lax.dynamic_slice_in_dim(
        comb_all, lax.axis_index("dp") * (experts * capacity), experts * capacity
    )
    back_grad, back_comb = (
        lax.all_to_all(
            summed.reshape(experts, capacity, width).astype(jnp.bfloat16),
            "expert",
            split_axis=0,
            concat_axis=0,
            tiled=True,
        ).astype(jnp.float32),
        lax.all_to_all(
            own_terms.reshape(experts, capacity).astype(jnp.bfloat16),
            "expert",
            split_axis=0,
            concat_axis=0,
            tiled=True,
        ).astype(jnp.float32),
    )
    placed = slot_table(expert_ids.reshape(-1), experts, capacity)
    owner = token_owner(placed, tokens, picks).astype(jnp.float32)
    grad_in = lax.dot_general(
        owner,
        back_grad.reshape(experts * capacity, width),
        (((0,), (0,)), ((), ())),
        precision=lax.Precision.HIGHEST,
    ).astype(jnp.bfloat16)
    grad_combine = lax.dot_general(
        placed.astype(jnp.float32),
        back_comb.reshape(experts * capacity),
        (((0,), (0,)), ((), ())),
        precision=lax.Precision.HIGHEST,
    ).reshape(tokens, picks)
    return (grad_in, grad_combine, grad_gate[None], grad_up[None], grad_down[None])


def solution(mesh):
    in_specs = (
        P(("dp", "expert"), None),
        P(("dp", "expert"), None),
        P(("dp", "expert"), None),
        P(("dp", "expert"), None),
        P(("dp", "expert"), None),
        P("expert", "dp", None),
        P("expert", "dp", None),
        P("expert", "dp", None),
    )
    out_specs = (
        P(("dp", "expert"), None),
        P(("dp", "expert"), None),
        P("expert", "dp", None),
        P("expert", "dp", None),
        P("expert", "dp", None),
    )
    return jax.shard_map(body, mesh=mesh, in_specs=in_specs, out_specs=out_specs, check_vma=False)
```

profile of v0, /device:TPU:0, one launch (start us, length us, event | category | flops | bytes accessed | tf_op | source)
XLA Modules:
  0.0 187.8 jit_solution(2804503160800750998)
XLA Ops:
  8.9 1.3 convolution_convert_fusion.3
  10.2 32.1 %all_to_all.36 = bf16[16,16,2048]{2,1,0:T(8,128)(2,1)} all-to-all(bf16[16,16,2048]{2,1,0:T(8,128)(2,1)S(1)} %bitcast.53), channel_id=1, replica_groups=mesh['dp'=2,'expert'=16] {'expert'}, dimensions={0} | all-to-all | bytes 2097152 | tf_op jit(solution)/shard_map/all_to_all | solution.py:50
  42.9 29.8 %all_to_all.37 = bf16[16,16,2048]{2,1,0:T(8,128)(2,1)} all-to-all(bf16[16,16,2048]{2,1,0:T(8,128)(2,1)S(1)} %bitcast.54), channel_id=1, replica_groups=mesh['dp'=2,'expert'=16] {'expert'}, dimensions={0} | all-to-all | bytes 2097152 | tf_op jit(solution)/shard_map/all_to_all | solution.py:49
  73.7 5.0 %all-to-all-start = ((bf16[16,1,16]{2,1,0:T(2,128)(2,1)}), bf16[16,1,16]{2,1,0:T(2,128)(2,1)S(1)}, u32[]{:S(2)}, u32[]{:S(2)}) async-start(bf16[16,1,16]{2,1,0:T(2,128)(2,1)} %all_to_all.29), calls=%async_computation | async-start | bytes 16384 | tf_op jit(solution)/shard_map/all_to_all | solution.py:52
  79.8 5.3 %all-to-all-done = bf16[16,1,16]{2,1,0:T(2,128)(2,1)S(1)} async-done(((bf16[16,1,16]{2,1,0:T(2,128)(2,1)}), bf16[16,1,16]{2,1,0:T(2,128)(2,1)S(1)}, u32[]{:S(2)}, u32[]{:S(2)}) %all-to-all-start) | async-done | bytes 544 | tf_op jit(solution)/shard_map/all_to_all | solution.py:52
  85.1 3.5 %all-to-all-start.3 = ((bf16[16,2,128]{2,1,0:T(2,128)(2,1)}), bf16[16,2,128]{2,1,0:T(2,128)(2,1)S(1)}, u32[]{:S(2)}, u32[]{:S(2)}) async-start(bf16[16,2,128]{2,1,0:T(2,128)(2,1)} %reshape.155), calls=%async_computation.3 | async-start | bytes 16384 | tf_op jit(solution)/shard_map/all_to_all | solution.py:51
  88.6 4.4 %all-gather = bf16[32,1,16]{2,0,1:T(8,128)(2,1)S(1)} all-gather(bf16[16,1,16]{2,0,1:T(8,128)(2,1)S(1)} %copy.63), channel_id=2, replica_groups=mesh['dp'=2,'expert'=16] {'dp'}, dimensions={0}, use_global_device_ids=true | all-gather | bytes 1536 | tf_op jit(solution)/shard_map/all_gather | solution.py:58
  93.1 1.7 all-to-all-done.3
  95.1 6.6 %all-gather.3 = bf16[32,16,16]{2,1,0:T(8,128)(2,1)S(1)} all-gather(bf16[16,16,16]{2,1,0:T(8,128)(2,1)S(1)} %copy.65), channel_id=5, replica_groups=mesh['dp'=2,'expert'=16] {'dp'}, dimensions={0}, use_global_device_ids=true | all-gather | bytes 24576 | tf_op jit(solution)/shard_map/all_gather | solution.py:57
  103.6 1.9 %fusion = bf16[512,2048]{1,0:T(8,128)(2,1)S(1)} fusion(f32[64,8,16,128]{3,2,1,0:T(8,128)S(1)} %bitcast.51, bf16[32,16,2048]{2,1,0:T(8,128)(2,1)S(1)} %copy-done.1), kind=kLoop, calls=%fused_computation.1 | loop fusion | flops 3145728 | bytes 8388608 | tf_op jit(solution)/shard_map/convert_element_type | solution.py:69
  105.6 1.3 copy-done.2
  106.9 3.0 %fusion.3 = f32[512,768]{0,1:T(8,128)} fusion(bf16[512,2048]{1,0:T(8,128)(2,1)S(1)} %fusion, bf16[384,2048]{1,0:T(8,128)(2,1)S(1)} %bitcast.63, bf16[384,2048]{1,0:T(8,128)(2,1)S(1)} %bitcast.65), kind=kOutput, calls=%fused_computation.12 | convolution fusion | flops 1616904192 | bytes 6815744 | tf_op jit(solution)/shard_map/dot_general | solution.py:75
  109.9 2.3 %all-gather.7.cloned.1.call-done = bf16[32,16,2048]{2,1,0:T(8,128)(2,1)} async-done(((bf16[16,16,2048]{2,1,0:T(8,128)(2,1)}), bf16[32,16,2048]{2,1,0:T(8,128)(2,1)}) %all-gather.7.cloned.1.call-update) | async-done | bytes 2097168 | tf_op jit(solution)/shard_map/all_gather | solution.py:55
  112.1 4.2 %multiply_reduce_fusion = (f32[512]{0:T(512)S(1)}, bf16[512,384]{0,1:T(8,128)(2,1)}, bf16[512,384]{0,1:T(8,128)(2,1)S(1)}, bf16[512,384]{0,1:T(8,128)(2,1)S(1)}) fusion(f32[512,768]{0,1:T(8,128)} %fusion.3, f32[512]{0:T(512)S(1)} %reshape.134, bf16[512,2048]{1,0:T(8,128)(2,1)} %bitcast.61, bf16[1,384,2048]{2,1,0:T(8,128)(2,1)S(1)} %copy-done), kind=kOutput, calls=%fused_computation.19 | convolution fusion | flops 809041408 | bytes 6426624 | tf_op jit(solution)/shard_map/dot_general | solution.py:84
  116.3 3.2 %convolution_convert_fusion.1 = bf16[512,2048]{1,0:T(8,128)(2,1)} fusion(bf16[384,2048]{1,0:T(8,128)(2,1)S(1)} %bitcast.64, bf16[384,2048]{1,0:T(8,128)(2,1)S(1)} %bitcast.66, bf16[512,384]{0,1:T(8,128)(2,1)S(1)} %get-tuple-element.11, bf16[512,384]{0,1:T(8,128)(2,1)S(1)} %get-tuple-element.12), kind=kOutput, calls=%fused_computation.5 | convolution fusion | flops 1619525632 | bytes 6029312 | tf_op jit(solution)/shard_map/dot_general | solution.py:102
  119.5 5.1 %psum.7 = bf16[512]{0:T(512)(128)(2,1)S(1)} all-reduce(f32[512]{0:T(512)S(1)} %get-tuple-element.5), channel_id=1, replica_groups=mesh['dp'=2,'expert'=16] {'dp'}, use_global_device_ids=true, to_apply=%region_5.6 | all-reduce | flops 512 | bytes 3072 | tf_op jit(solution)/shard_map/psum | solution.py:109
  124.8 11.8 %all_to_all.38 = bf16[16,1,16]{2,1,0:T(2,128)(2,1)S(1)} all-to-all(bf16[16,1,16]{2,1,0:T(2,128)(2,1)S(1)} %convert_element_type.147), channel_id=1, replica_groups=mesh['dp'=2,'expert'=16] {'expert'}, dimensions={0} | all-to-all | bytes 1024 | tf_op jit(solution)/shard_map/all_to_all | solution.py:121
  136.6 14.9 %reduce-scatter.2.cloned.1.call-done = bf16[1,16,16,2048]{3,2,1,0:T(8,128)(2,1)} async-done(((bf16[2,16,16,2048]{3,2,1,0:T(8,128)(2,1)}), bf16[1,16,16,2048]{3,2,1,0:T(8,128)(2,1)}) %reduce-scatter.2.cloned.1.call-update) | async-done | bytes 1048592 | tf_op jit(solution)/shard_map/reduce_scatter | solution.py:103
  151.5 5.6 %all-to-all-start.4 = ((bf16[16,16,2048]{2,1,0:T(8,128)(2,1)}), bf16[16,16,2048]{2,1,0:T(8,128)(2,1)S(1)}, u32[]{:S(2)}, u32[]{:S(2)}) async-start(bf16[16,16,2048]{2,1,0:T(8,128)(2,1)} %bitcast.57), calls=%async_computation.5 | async-start | bytes 2097152 | tf_op jit(solution)/shard_map/all_to_all | solution.py:114
  157.2 4.0 %fusion.1 = bf16[1,384,2048]{2,1,0:T(8,128)(2,1)} fusion(bf16[512,384]{0,1:T(8,128)(2,1)S(1)} %copy-done.10, bf16[512,2048]{1,0:T(8,128)(2,1)} %bitcast.62, f32[512]{0:T(512)S(1)} %reshape.134), kind=kOutput, calls=%fused_computation.7 | convolution fusion | flops 809238528 | bytes 4065280 | tf_op jit(solution)/shard_map/dot_general | solution.py:94
  161.2 1.8 convolution_convert_fusion
  163.0 2.0 %slice_bitcast_fusion = (bf16[1,384,2048]{2,1,0:T(8,128)(2,1)}, bf16[1,384,2048]{2,1,0:T(8,128)(2,1)}) fusion(bf16[768,2048]{1,0:T(8,128)(2,1)S(1)} %convolution_convert_fusion), kind=kLoop, calls=%fused_computation.13 | loop fusion | bytes 6291456 | tf_op jit(solution)/shard_map/broadcast_in_dim | solution.py:143
  166.2 13.9 %all-to-all-done.4 = bf16[16,16,2048]{2,1,0:T(8,128)(2,1)S(1)} async-done(((bf16[16,16,2048]{2,1,0:T(8,128)(2,1)}), bf16[16,16,2048]{2,1,0:T(8,128)(2,1)S(1)}, u32[]{:S(2)}, u32[]{:S(2)}) %all-to-all-start.4) | async-done | bytes 1048608 | tf_op jit(solution)/shard_map/all_to_all | solution.py:114
  180.1 1.2 convolution_convert_fusion.5
  (68 shorter events, 7.9 us)
Async XLA Ops:
  7.2 105.0 %copy-start = (bf16[1,384,2048]{2,1,0:T(8,128)(2,1)S(1)}, bf16[1,384,2048]{2,1,0:T(8,128)(2,1)}, u32[]{:S(2)}) copy-start(bf16[1,384,2048]{2,1,0:T(8,128)(2,1)} %param.15) | copy-start | bytes 4718596
  7.2 94.9 %all-gather.9.cloned.1.call-start = ((), (), s32[]{:S(2)}) async-start(), calls=%async_computation.9 | async-start | bytes 3145728 | tf_op jit(solution)/shard_map/all_gather | solution.py:56
  8.9 33.6 %copy-start.4 = (bf16[16,2048]{1,0:T(8,128)(2,1)S(1)}, bf16[16,2048]{1,0:T(8,128)(2,1)}, u32[]{:S(2)}) copy-start(bf16[16,2048]{1,0:T(8,128)(2,1)} %param.8) | copy-start | bytes 196612
  42.4 30.3 %copy-start.5 = (bf16[16,8]{0,1:T(8,128)(2,1)S(1)}, bf16[16,8]{0,1:T(8,128)(2,1)}, u32[]{:S(2)}) copy-start(bf16[16,8]{0,1:T(8,128)(2,1)} %param.11) | copy-start | bytes 772
  42.4 36.4 %copy-start.9 = (bf16[16,16]{1,0:T(8,128)(2,1)S(1)}, bf16[16,16]{1,0:T(8,128)(2,1)}, u32[]{:S(2)}) copy-start(bf16[16,16]{1,0:T(8,128)(2,1)} %param.10) | copy-start | bytes 1540
  42.4 69.7 %all-gather.7.cloned.1.call-start = ((), (), s32[]{:S(2)}) async-start(), calls=%async_computation.8 | async-start | bytes 3145728 | tf_op jit(solution)/shard_map/all_gather | solution.py:55
  73.7 11.3 %all-to-all-start = ((bf16[16,1,16]{2,1,0:T(2,128)(2,1)}), bf16[16,1,16]{2,1,0:T(2,128)(2,1)S(1)}, u32[]{:S(2)}, u32[]{:S(2)}) async-start(bf16[16,1,16]{2,1,0:T(2,128)(2,1)} %all_to_all.29), calls=%async_computation | async-start | bytes 16384 | tf_op jit(solution)/shard_map/all_to_all | solution.py:52
  85.1 9.8 %all-to-all-start.3 = ((bf16[16,2,128]{2,1,0:T(2,128)(2,1)}), bf16[16,2,128]{2,1,0:T(2,128)(2,1)S(1)}, u32[]{:S(2)}, u32[]{:S(2)}) async-start(bf16[16,2,128]{2,1,0:T(2,128)(2,1)} %reshape.155), calls=%async_computation.3 | async-start | bytes 16384 | tf_op jit(solution)/shard_map/all_to_all | solution.py:51
  88.6 63.0 %reduce-scatter.2.cloned.1.call-start = ((), (), s32[]{:S(2)}) async-start(), calls=%async_computation.7 | async-start | bytes 3145728 | tf_op jit(solution)/shard_map/reduce_scatter | solution.py:103
  102.0 1.6 copy-start.1
  103.6 3.3 %copy-start.6 = (bf16[1,384,2048]{2,1,0:T(8,128)(2,1)S(1)}, bf16[1,384,2048]{2,1,0:T(8,128)(2,1)}, u32[]{:S(2)}) copy-start(bf16[1,384,2048]{2,1,0:T(8,128)(2,1)} %param.14) | copy-start | bytes 4718596
  103.6 3.3 %copy-start.7 = (bf16[1,384,2048]{2,1,0:T(8,128)(2,1)S(1)}, bf16[1,384,2048]{2,1,0:T(8,128)(2,1)}, u32[]{:S(2)}) copy-start(bf16[1,384,2048]{2,1,0:T(8,128)(2,1)} %param.13) | copy-start | bytes 4718596
  105.6 1.3 copy-start.2
  112.1 4.2 %copy-start.8 = (bf16[1,384,2048]{2,1,0:T(8,128)(2,1)S(1)}, bf16[1,384,2048]{2,1,0:T(8,128)(2,1)}, u32[]{:S(2)}) copy-start(bf16[1,384,2048]{2,1,0:T(8,128)(2,1)} %param.13) | copy-start | bytes 4718596
  116.3 3.2 %copy-start.11 = (bf16[512,384]{0,1:T(8,128)(2,1)}, bf16[512,384]{0,1:T(8,128)(2,1)S(1)}, u32[]{:S(2)}) copy-start(bf16[512,384]{0,1:T(8,128)(2,1)S(1)} %get-tuple-element.11) | copy-start | bytes 1179652
  116.3 3.2 %copy-start.13 = (bf16[512,384]{0,1:T(8,128)(2,1)}, bf16[512,384]{0,1:T(8,128)(2,1)S(1)}, u32[]{:S(2)}) copy-start(bf16[512,384]{0,1:T(8,128)(2,1)S(1)} %get-tuple-element.12) | copy-start | bytes 1179652
  119.5 37.6 %copy-start.10 = (bf16[512,384]{0,1:T(8,128)(2,1)S(1)}, bf16[512,384]{0,1:T(8,128)(2,1)}, u32[]{:S(2)}) copy-start(bf16[512,384]{0,1:T(8,128)(2,1)} %get-tuple-element.6) | copy-start | bytes 1179652
  151.5 28.6 %all-to-all-start.4 = ((bf16[16,16,2048]{2,1,0:T(8,128)(2,1)}), bf16[16,16,2048]{2,1,0:T(8,128)(2,1)S(1)}, u32[]{:S(2)}, u32[]{:S(2)}) async-start(bf16[16,16,2048]{2,1,0:T(8,128)(2,1)} %bitcast.57), calls=%async_computation.5 | async-start | bytes 2097152 | tf_op jit(solution)/shard_map/all_to_all | solution.py:114
  157.2 4.0 %copy-start.3 = (bf16[512,2048]{1,0:T(8,128)(2,1)S(1)}, bf16[512,2048]{1,0:T(8,128)(2,1)}, u32[]{:S(2)}) copy-start(bf16[512,2048]{1,0:T(8,128)(2,1)} %copy-done.2) | copy-start | bytes 6291460
  157.2 4.0 %copy-start.12 = (bf16[512,384]{0,1:T(8,128)(2,1)S(1)}, bf16[512,384]{0,1:T(8,128)(2,1)}, u32[]{:S(2)}) copy-start(bf16[512,384]{0,1:T(8,128)(2,1)} %copy-done.11) | copy-start | bytes 1179652
  157.2 4.0 %copy-start.14 = (bf16[512,384]{0,1:T(8,128)(2,1)S(1)}, bf16[512,384]{0,1:T(8,128)(2,1)}, u32[]{:S(2)}) copy-start(bf16[512,384]{0,1:T(8,128)(2,1)} %copy-done.13) | copy-start | bytes 1179652
Sparse Core Ops, SparseCore 0:
  42.5 33.4 all-gather.8
  77.5 34.5 all-gather.6
  119.6 31.8 reduce-scatter.1
where the time goes:
time: 189 us; the launch traced here: 188 us
  blocking collectives  89.8 us (48%)
  waiting for transfers between devices  38.2 us (20%)
  matrix products  19.7 us (10%)
  starting transfers between devices  14.2 us (8%)
  between operations  14 us (7%)
  local copies, waits for them, and re-layouts  9.29 us (5%)
  other arithmetic  2.54 us (1%)
    all_to_all x1, blocking collectives, body(): lax.all_to_all(code_rows, 'expert', split_axis=0, concat_axis=0, tiled=True)  32.1 us
    all_to_all x1, blocking collectives, body(): lax.all_to_all(grad_rows, 'expert', split_axis=0, concat_axis=0, tiled=True)  29.8 us
    reduce_scatter x1, waiting for transfers between devices, body(): lax.psum_scatter(input_part.reshape(groups, experts, capacity, width).ast...  14.9 us
    all_to_all x1, waiting for transfers between devices, body(): lax.all_to_all(summed.reshape(experts, capacity, width).astype(jnp.bfloat...  13.9 us
    all_to_all x1, blocking collectives, body(): lax.all_to_all(own_terms.reshape(experts, capacity).astype(jnp.bfloat16),...  11.8 us
    all_gather x1, blocking collectives, body(): lax.all_gather(scale_rows[None], 'dp', axis=0, tiled=True)  6.61 us
    all_to_all x1, starting transfers between devices, body(): lax.all_to_all(summed.reshape(experts, capacity, width).astype(jnp.bfloat...  5.63 us
    all_to_all x1, waiting for transfers between devices, body(): lax.all_to_all(weight_rows, 'expert', split_axis=0, concat_axis=0, tiled=...  5.29 us
  transfers between devices with their start and end apart: 6, of which 5 were waited for; matrix products, arithmetic and copies ran while one was open for 9% of the time, Pallas kernels for 0%

commit v1 on v0

--- a/solution.py
+++ b/solution.py
@@ -143,6 +143,75 @@
     return (grad_in, grad_combine, grad_gate[None], grad_up[None], grad_down[None])
 
 
+def dense_body(grad_out, x_codes, x_scales, combine, expert_ids, w_gate, w_up, w_down):
+    tokens, picks = expert_ids.shape
+    width = grad_out.shape[1]
+    experts = w_gate.shape[0] * lax.axis_size("expert")
+    axes = ("dp", "expert")
+    lanes = -(-experts // BLOCK) * BLOCK
+    x_own = (
+        (
+            x_codes.reshape(tokens, -1, BLOCK).astype(jnp.float32)
+            * x_scales.reshape(tokens, -1, 1).astype(jnp.float32)
+        )
+        .reshape(tokens, width)
+        .astype(jnp.bfloat16)
+    )
+    picked = expert_ids[:, :, None] == jnp.arange(lanes, dtype=jnp.int32)[None, None, :]
+    weight_own = jnp.sum(
+        jnp.where(picked, combine[:, :, None].astype(jnp.float32), 0.0), axis=1
+    ).astype(jnp.bfloat16)
+    packed = jnp.concatenate([grad_out, x_own, weight_own], axis=1)
+    every = lax.all_gather(packed, axes, axis=0, tiled=True)
+    grad_rows = every[:, :width]
+    x_rows = every[:, width : 2 * width]
+    mine = jnp.arange(lanes)[None, :] == lax.axis_index("expert")
+    weight = jnp.sum(jnp.where(mine, every[:, 2 * width :].astype(jnp.float32), 0.0), axis=1)[:, None]
+    contract = (((1,), (1,)), ((), ()))
+    over_rows = (((0,), (0,)), ((), ()))
+    f32 = jnp.float32
+    gate_pre = lax.dot_general(x_rows, w_gate[0], contract, preferred_element_type=f32)
+    up_pre = lax.dot_general(x_rows, w_up[0], contract, preferred_element_type=f32)
+    backward = lax.dot_general(grad_rows, w_down[0], contract, preferred_element_type=f32)
+    sigmoid_gate = jax.nn.sigmoid(gate_pre)
+    activated = gate_pre * sigmoid_gate
+    hidden = (activated * up_pre).astype(jnp.bfloat16)
+    scaled = (weight * grad_rows.astype(f32)).astype(jnp.bfloat16)
+    comb = jnp.sum(backward * hidden.astype(f32), axis=1)[:, None]
+    grad_hidden = weight * backward
+    grad_gate_pre = (
+        grad_hidden * up_pre * sigmoid_gate * (1.0 + gate_pre * (1.0 - sigmoid_gate))
+    ).astype(jnp.bfloat16)
+    grad_up_pre = (grad_hidden * activated).astype(jnp.bfloat16)
+    input_part = jnp.dot(grad_gate_pre, w_gate[0], preferred_element_type=f32) + jnp.dot(
+        grad_up_pre, w_up[0], preferred_element_type=f32
+    )
+    terms = jnp.concatenate([input_part, jnp.where(mine, comb, 0.0)], axis=1).astype(jnp.bfloat16)
+    summed = lax.psum_scatter(terms, axes, scatter_dimension=0, tiled=True)
+    grad_down = lax.dot_general(hidden, scaled, over_rows, preferred_element_type=f32)
+    grad_gate = lax.dot_general(grad_gate_pre, x_rows, over_rows, preferred_element_type=f32)
+    grad_up = lax.dot_general(grad_up_pre, x_rows, over_rows, preferred_element_type=f32)
+    grad_in = summed[:, :width]
+    grad_combine = jnp.sum(
+        jnp.where(picked, summed[:, None, width:].astype(f32), 0.0), axis=2
+    )
+    return (
+        grad_in,
+        grad_combine,
+        grad_gate.astype(jnp.bfloat16)[None],
+        grad_up.astype(jnp.bfloat16)[None],
+        grad_down.astype(jnp.bfloat16)[None],
+    )
+
+
+def chosen_body(grad_out, x_codes, x_scales, combine, expert_ids, w_gate, w_up, w_down):
+    tokens, picks = expert_ids.shape
+    experts = w_gate.shape[0] * lax.axis_size("expert")
+    capacity = min(tokens, max(2, 2 * tokens * picks // experts))
+    chosen = dense_body if capacity == tokens and w_gate.shape[0] == 1 else body
+    return chosen(grad_out, x_codes, x_scales, combine, expert_ids, w_gate, w_up, w_down)
+
+
 def solution(mesh):
     in_specs = (
         P(("dp", "expert"), None),
@@ -161,4 +230,4 @@
         P("expert", "dp", None),
         P("expert", "dp", None),
     )
-    return jax.shard_map(body, mesh=mesh, in_specs=in_specs, out_specs=out_specs, check_vma=False)
+    return jax.shard_map(chosen_body, mesh=mesh, in_specs=in_specs, out_specs=out_specs, check_vma=False)

time: 189 us -> 235 us (1.24)
  waiting for transfers between devices: 38.2 us -> 190 us
  blocking collectives: 89.8 us -> 0 us
  starting transfers between devices: 14.2 us -> 0.08 us
  local copies, waits for them, and re-layouts: 9.29 us -> 5.51 us
  other arithmetic: 2.54 us -> 6.09 us
    reduce_scatter x1, waiting for transfers between devices: 14.9 us -> 124 us  [dense_body(): summed = lax.psum_scatter(terms, axes, scatter_dimension=0, tiled=True)]
    all_to_all x3 -> x0, blocking collectives: 73.7 us -> none  [the longest x1 32.1 us: body(): lax.all_to_all(code_rows, 'expert', split_axis=0, concat_axis=0, tiled=True)]
    all_gather x2 -> x1, waiting for transfers between devices: 2.28 us -> 65.3 us  [dense_body(): every = lax.all_gather(packed, axes, axis=0, tiled=True)]
    all_to_all x3 -> x0, waiting for transfers between devices: 21 us -> none  [the longest x1 13.9 us: body(): lax.all_to_all(summed.reshape(experts, capacity, width).astype(jnp.bfloat...]
    all_to_all x3 -> x0, starting transfers between devices: 14.1 us -> none  [the longest x1 5.63 us: body(): lax.all_to_all(summed.reshape(experts, capacity, width).astype(jnp.bfloat...]
    all_gather x2 -> x0, blocking collectives: 11 us -> none  [the longest x1 6.61 us: body(): lax.all_gather(scale_rows[None], 'dp', axis=0, tiled=True)]
    psum x1 -> x0, blocking collectives: 5.08 us -> none  [body(): comb_all = lax.psum(partial_comb, 'dp')]
    concatenate x0 -> x2, other arithmetic: none -> 3.08 us  [the longest x1 1.57 us: dense_body(): jnp.concatenate([input_part, jnp.where(mine, comb, 0.0)], axis=1)]
  transfers between devices with their start and end apart: 6 -> 2, of which waited for: 5 -> 2; matrix products, arithmetic and copies ran while one was open for 9% -> 5% of each run, Pallas kernels for 0% -> 0%
where the time goes in v1:
time: 235 us
  waiting for transfers between devices  190 us (81%)
  matrix products  19 us (8%)
  between operations  14.1 us (6%)
  other arithmetic  6.09 us (3%)
  local copies, waits for them, and re-layouts  5.51 us (2%)
    reduce_scatter x1, waiting for transfers between devices, dense_body(): summed = lax.psum_scatter(terms, axes, scatter_dimension=0, tiled=True)  124 us
    all_gather x1, waiting for transfers between devices, dense_body(): every = lax.all_gather(packed, axes, axis=0, tiled=True)  65.3 us
  transfers between devices with their start and end apart: 2, of which 2 were waited for; matrix products, arithmetic and copies ran while one was open for 5% of the time, Pallas kernels for 0%

profile of v1, /device:TPU:0, one launch (start us, length us, event | category | flops | bytes accessed | tf_op | source)
XLA Modules:
  0.0 234.6 jit_solution(13662257801595468613)
XLA Ops:
  7.2 0.9 copy.15
  8.1 0.8 copy.16
  9.0 0.8 mul.51
  9.7 0.9 fusion.20
  10.6 1.5 pad_maximum_fusion.1
  12.2 65.3 %all-gather.2.cloned.1.call-done = bf16[512,4224]{1,0:T(8,128)(2,1)} async-done(((bf16[16,4224]{1,0:T(8,128)(2,1)}), bf16[512,4224]{1,0:T(8,128)(2,1)}) %all-gather.2.cloned.1.call-update) | async-done | bytes 4325392 | tf_op jit(solution)/shard_map/all_gather | solution.py:165
  77.5 1.0 select_reduce_fusion
  78.6 2.8 %fusion.9 = f32[512,384]{0,1:T(8,128)S(1)} fusion(bf16[1,384,2048]{2,1,0:T(8,128)(2,1)S(1)} %copy-done, bf16[512,4224]{1,0:T(8,128)(2,1)} %all-gather.2.cloned.1.call-done), kind=kOutput, calls=%fused_computation.15 | convolution fusion | flops 805306368 | bytes 4456448 | tf_op jit(solution)/shard_map/dot_general | solution.py:173
  81.4 0.6 copy-done.2
  81.9 1.0 fusion.12
  82.9 0.4 copy-done.3
  83.3 1.4 multiply_reduce_fusion
  84.7 0.1 select_convert_fusion
  84.8 1.3 fusion.7
  86.1 1.3 add_convert_fusion
  87.4 1.6 pad_maximum_fusion
  89.0 3.7 %fusion = bf16[1,384,2048]{2,1,0:T(8,128)(2,1)} fusion(bf16[512,384]{0,1:T(8,128)(2,1)S(1)} %get-tuple-element.12, bf16[512,4224]{1,0:T(8,128)(2,1)} %all-gather.2.cloned.1.call-done), kind=kOutput, calls=%fused_computation.5 | convolution fusion | flops 806092800 | bytes 4063232 | tf_op jit(solution)/shard_map/dot_general | solution.py:192
  92.8 3.7 %fusion.1 = bf16[1,384,2048]{2,1,0:T(8,128)(2,1)} fusion(bf16[512,384]{0,1:T(8,128)(2,1)S(1)} %get-tuple-element.13, bf16[512,4224]{1,0:T(8,128)(2,1)} %all-gather.2.cloned.1.call-done), kind=kOutput, calls=%fused_computation.6 | convolution fusion | flops 806092800 | bytes 4063232 | tf_op jit(solution)/shard_map/dot_general | solution.py:193
  96.5 3.8 %fusion.2 = bf16[1,384,2048]{2,1,0:T(8,128)(2,1)} fusion(bf16[512,384]{0,1:T(8,128)(2,1)S(1)} %get-tuple-element.11, f32[512]{0:T(512)S(1)} %select_reduce_fusion, bf16[512,4224]{1,0:T(8,128)(2,1)} %all-gather.2.cloned.1.call-done), kind=kOutput, calls=%fused_computation.7 | convolution fusion | flops 809238528 | bytes 4065280 | tf_op jit(solution)/shard_map/dot_general | solution.py:191
  100.3 124.4 %reduce-scatter.2.cloned.1.call-done = bf16[16,2176]{1,0:T(8,128)(2,1)} async-done(((bf16[512,2176]{1,0:T(8,128)(2,1)}), bf16[16,2176]{1,0:T(8,128)(2,1)}) %reduce-scatter.2.cloned.1.call-update) | async-done | bytes 69648 | tf_op jit(solution)/shard_map/reduce_scatter | solution.py:190
  224.7 0.7 slice_convert_fusion
  225.4 0.2 select_reduce_fusion.1
  225.6 0.7 copy.17
  226.2 1.5 slice.23
  (12 shorter events, 0.3 us)
Async XLA Ops:
  7.2 71.4 %copy-start = (bf16[1,384,2048]{2,1,0:T(8,128)(2,1)S(1)}, bf16[1,384,2048]{2,1,0:T(8,128)(2,1)}, u32[]{:S(2)}) copy-start(bf16[1,384,2048]{2,1,0:T(8,128)(2,1)} %param.13) | copy-start | bytes 4718596
  7.2 70.4 %all-gather.2.cloned.1.call-start = ((), (), s32[]{:S(2)}) async-start(), calls=%async_computation.1 | async-start | bytes 4460544 | tf_op jit(solution)/shard_map/all_gather | solution.py:165
  12.2 212.6 %reduce-scatter.2.cloned.1.call-start = ((), (), s32[]{:S(2)}) async-start(), calls=%async_computation.2 | async-start | bytes 2297856 | tf_op jit(solution)/shard_map/reduce_scatter | solution.py:190
  78.6 2.8 %copy-start.1 = (bf16[1,384,2048]{2,1,0:T(8,128)(2,1)S(1)}, bf16[1,384,2048]{2,1,0:T(8,128)(2,1)}, u32[]{:S(2)}) copy-start(bf16[1,384,2048]{2,1,0:T(8,128)(2,1)} %param.14) | copy-start | bytes 4718596
  78.6 3.3 %copy-start.2 = (bf16[512,4224]{1,0:T(8,128)(2,1)S(1)}, bf16[512,4224]{1,0:T(8,128)(2,1)}, u32[]{:S(2)}) copy-start(bf16[512,4224]{1,0:T(8,128)(2,1)} %all-gather.2.cloned.1.call-done) | copy-start | bytes 12976132
  81.9 1.4 copy-start.3
Sparse Core Ops, SparseCore 0:
  12.3 65.2 all-gather.1
  89.2 135.5 reduce-scatter.1

commit v2 on v0

--- a/solution.py
+++ b/solution.py
@@ -1,9 +1,14 @@
+import functools
+
 import jax
 import jax.numpy as jnp
 from jax import lax
+from jax.experimental import pallas as pl
+from jax.experimental.pallas import tpu as pltpu
 from jax.sharding import PartitionSpec as P
 
 BLOCK = 128
+MESH = pl.DeviceIdType.MESH
 
 
 def slot_table(flat_ids, experts, capacity):
@@ -143,6 +148,377 @@
     return (grad_in, grad_combine, grad_gate[None], grad_up[None], grad_down[None])
 
 
+def expert_kernel(
+    tokens,
+    width,
+    share,
+    lanes,
+    picks,
+    grad_ref,
+    codes_ref,
+    scales_ref,
+    combine_ref,
+    ids_ref,
+    gate_hbm,
+    up_hbm,
+    down_hbm,
+    grad_in_ref,
+    comb_ref,
+    grad_gate_hbm,
+    grad_up_hbm,
+    grad_down_hbm,
+    rows_buf,
+    stack_w,
+    down_w,
+    pre_buf,
+    back_buf,
+    act_buf,
+    hid_buf,
+    act_t,
+    hid_t,
+    stack_out,
+    down_out,
+    terms,
+    from_sib,
+    from_first,
+    from_second,
+    from_z,
+    send_sems,
+    row_sems,
+    sib_sems,
+    first_sems,
+    second_sem,
+    z_sems,
+    local_sems,
+):
+    f32, bf16 = jnp.float32, jnp.bfloat16
+    half_rows, fam_rows, group_rows = 16 * tokens, 8 * tokens, 4 * tokens
+    x = lax.axis_index("dp")
+    place = lax.axis_index("expert")
+    z, y, c = place // 4, (place // 2) % 2, place % 2
+
+    def device(dx, dz, dy, dc):
+        return (dx, dz * 4 + dy * 2 + dc)
+
+    sib = device(x, z, y, 1 - c)
+    first = device(x + (1 - c) * (1 - 2 * x), z, y + c * (1 - 2 * y), c)
+    second = device(x + c * (1 - 2 * x), z, y + (1 - c) * (1 - 2 * y), c)
+    peer_z = [z + 1 - 2 * (z % 2), z + 2 - 4 * (z // 2), 3 - z]
+    peers = [device(x, pz, y, c) for pz in peer_z]
+    other = x + c * (y - x)
+
+    in_copies = [
+        pltpu.make_async_copy(gate_hbm.at[0], stack_w.at[pl.ds(0, share)], local_sems.at[0]),
+        pltpu.make_async_copy(up_hbm.at[0], stack_w.at[pl.ds(share, share)], local_sems.at[1]),
+        pltpu.make_async_copy(down_hbm.at[0], down_w, local_sems.at[2]),
+    ]
+    for copy in in_copies:
+        copy.start()
+
+    barrier = pltpu.get_barrier_semaphore()
+    for partner in [sib, first, second] + peers:
+        pl.semaphore_signal(barrier, inc=1, device_id=partner, device_id_type=MESH)
+
+    def slot(half, fam, oth, zz):
+        return half * 16 + fam * 8 + oth * 4 + zz
+
+    def at_slot(index):
+        return pl.ds(pl.multiple_of(index * tokens, tokens), tokens)
+
+    own = slot(0, c, other, z)
+    own_rows = at_slot(own)
+    rows_buf[own_rows, 0:width] = grad_ref[...]
+    scales = scales_ref[...].astype(f32)
+    for b in range(width // BLOCK):
+        cols = slice(b * BLOCK, (b + 1) * BLOCK)
+        rows_buf[own_rows, width + b * BLOCK : width + (b + 1) * BLOCK] = (
+            codes_ref[:, cols].astype(f32) * scales[:, b : b + 1]
+        ).astype(bf16)
+    lane = lax.broadcasted_iota(jnp.int32, (tokens, lanes), 1)
+    combine = combine_ref[...].astype(f32)
+    ids = ids_ref[...]
+    weight_row = jnp.zeros((tokens, lanes), f32)
+    for k in range(picks):
+        weight_row += jnp.where(lane == ids[:, k : k + 1], combine[:, k : k + 1], 0.0)
+    rows_buf[own_rows, 2 * width :] = weight_row.astype(bf16)
+
+    pl.semaphore_wait(barrier, 6)
+
+    sent = []
+
+    def send(src, dst, sem, to):
+        copy = pltpu.make_async_remote_copy(
+            src_ref=src,
+            dst_ref=dst,
+            send_sem=send_sems.at[len(sent)],
+            recv_sem=sem,
+            device_id=to,
+            device_id_type=MESH,
+        )
+        copy.start()
+        sent.append(copy)
+
+    def arrived(ref, sem):
+        pltpu.make_async_remote_copy(
+            src_ref=ref,
+            dst_ref=ref,
+            send_sem=send_sems.at[0],
+            recv_sem=sem,
+            device_id=sib,
+            device_id_type=MESH,
+        ).wait_recv()
+
+    def send_rows(src, dst, to):
+        send(rows_buf.at[at_slot(src)], rows_buf.at[at_slot(dst)], row_sems.at[dst], to)
+
+    def rows_arrived(index):
+        arrived(rows_buf.at[at_slot(index)], row_sems.at[index])
+
+    every_z = [z] + peer_z
+    send_rows(own, own, first)
+    for peer in peers:
+        send_rows(own, own, peer)
+    send_rows(own, own + 16, second)
+    send_rows(own, own, sib)
+    for pz in peer_z:
+        here = slot(0, c, other, pz)
+        rows_arrived(here)
+        send_rows(here, here, first)
+        send_rows(here, here + 16, second)
+        send_rows(here, here, sib)
+    for pz in every_z:
+        here = slot(0, c, 1 - other, pz)
+        rows_arrived(here)
+        send_rows(here, here + 16, second)
+        send_rows(here, here, sib)
+    for oth in (other, 1 - other):
+        for pz in every_z:
+            rows_arrived(slot(0, 1 - c, oth, pz))
+    for copy in in_copies:
+        copy.wait()
+
+    contract = (((1,), (1,)), ((), ()))
+    strip = 2 * tokens
+    mine = lax.broadcasted_iota(jnp.int32, (strip, lanes), 1) == place
+
+    def compute(half):
+        base = half * half_rows
+        grad_rows = rows_buf[base : base + half_rows, 0:width]
+        x_rows = rows_buf[base : base + half_rows, width : 2 * width]
+        pre_buf[...] = lax.dot_general(
+            x_rows, stack_w[...], contract, preferred_element_type=f32
+        )
+        back_buf[...] = lax.dot_general(
+            grad_rows, down_w[...], contract, preferred_element_type=f32
+        )
+
+        def elementwise(i, carry):
+            at = pl.ds(pl.multiple_of(i * strip, strip), strip)
+            full = pl.ds(pl.multiple_of(base + i * strip, strip), strip)
+            weight = jnp.sum(
+                jnp.where(mine, rows_buf[full, 2 * width :].astype(f32), 0.0),
+                axis=1,
+                keepdims=True,
+            )
+            gate_pre = pre_buf[at, 0:share]
+            up_pre = pre_buf[at, share:]
+            backward = back_buf[at, :]
+            sigmoid_gate = jax.nn.sigmoid(gate_pre)
+            activated = gate_pre * sigmoid_gate
+            hidden = activated * up_pre
+            comb = jnp.sum(backward * hidden, axis=1, keepdims=True)
+            grad_hidden = weight * backward
+            act_buf[at, 0:share] = (
+                grad_hidden * up_pre * sigmoid_gate * (1.0 + gate_pre * (1.0 - sigmoid_gate))
+            ).astype(bf16)
+            act_buf[at, share:] = (grad_hidden * activated).astype(bf16)
+            hid_buf[at, :] = (weight * hidden).astype(bf16)
+            terms[full, width:] = jnp.where(mine, comb, 0.0).astype(bf16)
+            return carry
+
+        lax.fori_loop(0, half_rows // strip, elementwise, 0)
+        tile = 512
+
+        def back_tile(i, carry):
+            cols = pl.ds(pl.multiple_of(i * tile, tile), tile)
+            terms[base : base + half_rows, cols] = jnp.dot(
+                act_buf[...], stack_w[:, cols], preferred_element_type=f32
+            ).astype(bf16)
+            return carry
+
+        lax.fori_loop(0, width // tile, back_tile, 0)
+
+    def fam_at(half, fam):
+        return pl.ds(pl.multiple_of(half * half_rows + fam * fam_rows, fam_rows), fam_rows)
+
+    def group_at(half, oth):
+        return pl.ds(
+            pl.multiple_of(half * half_rows + c * fam_rows + oth * group_rows, group_rows),
+            group_rows,
+        )
+
+    def to_sib(half):
+        send(terms.at[fam_at(half, 1 - c)], from_sib.at[half], sib_sems.at[half], sib)
+
+    def transpose(half):
+        cols = slice(half * half_rows, (half + 1) * half_rows)
+        act_t[:, cols] = act_buf[...].T
+        hid_t[:, cols] = hid_buf[...].T
+
+    def add_group(half, oth, others):
+        def add(i, carry):
+            at = half * half_rows + c * fam_rows + oth * group_rows + i * tokens
+            at = pl.ds(pl.multiple_of(at, tokens), tokens)
+            sib_at = pl.ds(pl.multiple_of(oth * group_rows + i * tokens, tokens), tokens)
+            rest = pl.ds(pl.multiple_of(i * tokens, tokens), tokens)
+            total = terms[at, :].astype(f32) + from_sib[half, sib_at, :].astype(f32)
+            for ref in others:
+                total += ref[rest, :].astype(f32)
+            terms[at, :] = total.astype(bf16)
+            return carry
+
+        lax.fori_loop(0, 4, add, 0)
+
+    def to_first(half):
+        arrived(from_sib.at[half], sib_sems.at[half])
+        add_group(half, 1 - other, [])
+        send(terms.at[group_at(half, 1 - other)], from_first.at[half], first_sems.at[half], first)
+
+    def weight_tiles(left, right_start, out):
+        tile = 512
+
+        def step(i, carry):
+            cols = pl.ds(pl.multiple_of(i * tile, tile), tile)
+            right = pl.ds(pl.multiple_of(right_start + i * tile, BLOCK), tile)
+            out[:, cols] = jnp.dot(
+                left[...], rows_buf[:, right], preferred_element_type=f32
+            ).astype(bf16)
+            return carry
+
+        lax.fori_loop(0, width // tile, step, 0)
+
+    compute(0)
+    to_sib(0)
+    transpose(0)
+    for oth in (other, 1 - other):
+        for pz in every_z:
+            here = slot(1, c, oth, pz)
+            rows_arrived(here)
+            send_rows(here, here, sib)
+    to_first(0)
+    for oth in (other, 1 - other):
+        for pz in every_z:
+            rows_arrived(slot(1, 1 - c, oth, pz))
+    compute(1)
+    to_sib(1)
+    transpose(1)
+    weight_tiles(hid_t, 0, down_out)
+    out_copies = [pltpu.make_async_copy(down_out, grad_down_hbm.at[0], local_sems.at[3])]
+    out_copies[0].start()
+    to_first(1)
+    weight_tiles(act_t.at[pl.ds(0, share)], width, stack_out.at[pl.ds(0, share)])
+    out_copies.append(
+        pltpu.make_async_copy(stack_out.at[pl.ds(0, share)], grad_gate_hbm.at[0], local_sems.at[4])
+    )
+    out_copies[1].start()
+    for half in (1, 0):
+        arrived(from_first.at[half], first_sems.at[half])
+    add_group(1, other, [from_first.at[1]])
+    send(terms.at[group_at(1, other)], from_second, second_sem, second)
+    weight_tiles(act_t.at[pl.ds(share, share)], width, stack_out.at[pl.ds(share, share)])
+    out_copies.append(
+        pltpu.make_async_copy(
+            stack_out.at[pl.ds(share, share)], grad_up_hbm.at[0], local_sems.at[5]
+        )
+    )
+    out_copies[2].start()
+    arrived(from_second, second_sem)
+    add_group(0, other, [from_first.at[0], from_second])
+    for k in range(3):
+        send(
+            terms.at[at_slot(slot(0, c, other, peer_z[k]))], from_z.at[k], z_sems.at[k], peers[k]
+        )
+    for k in range(3):
+        arrived(from_z.at[k], z_sems.at[k])
+    total = terms[own_rows, :].astype(f32)
+    for k in range(3):
+        total += from_z[k].astype(f32)
+    grad_in_ref[...] = total[:, 0:width].astype(bf16)
+    place_k = lax.broadcasted_iota(jnp.int32, (tokens, picks), 1)
+    comb_out = jnp.zeros((tokens, picks), f32)
+    for k in range(picks):
+        value = jnp.sum(
+            jnp.where(lane == ids[:, k : k + 1], total[:, width:], 0.0), axis=1, keepdims=True
+        )
+        comb_out += jnp.where(place_k == k, value, 0.0)
+    comb_ref[...] = comb_out
+    for copy in sent:
+        copy.wait_send()
+    for copy in out_copies:
+        copy.wait()
+
+
+def fused_body(grad_out, x_codes, x_scales, combine, expert_ids, w_gate, w_up, w_down):
+    tokens, picks = expert_ids.shape
+    width, share = grad_out.shape[1], w_gate.shape[1]
+    experts = w_gate.shape[0] * lax.axis_size("expert")
+    lanes = -(-experts // BLOCK) * BLOCK
+    bf16, f32 = jnp.bfloat16, jnp.float32
+    back = width + lanes
+    vmem = pl.BlockSpec(memory_space=pltpu.VMEM)
+    hbm = pl.BlockSpec(memory_space=pl.ANY)
+    dma = pltpu.SemaphoreType.DMA
+    return pl.pallas_call(
+        functools.partial(expert_kernel, tokens, width, share, lanes, picks),
+        out_shape=(
+            jax.ShapeDtypeStruct(grad_out.shape, bf16),
+            jax.ShapeDtypeStruct(combine.shape, f32),
+            jax.ShapeDtypeStruct(w_gate.shape, bf16),
+            jax.ShapeDtypeStruct(w_up.shape, bf16),
+            jax.ShapeDtypeStruct(w_down.shape, bf16),
+        ),
+        in_specs=[vmem] * 5 + [hbm] * 3,
+        out_specs=(vmem, vmem, hbm, hbm, hbm),
+        scratch_shapes=[
+            pltpu.VMEM((32 * tokens, 2 * width + lanes), bf16),
+            pltpu.VMEM((2 * share, width), bf16),
+            pltpu.VMEM((share, width), bf16),
+            pltpu.VMEM((16 * tokens, 2 * share), f32),
+            pltpu.VMEM((16 * tokens, share), f32),
+            pltpu.VMEM((16 * tokens, 2 * share), bf16),
+            pltpu.VMEM((16 * tokens, share), bf16),
+            pltpu.VMEM((2 * share, 32 * tokens), bf16),
+            pltpu.VMEM((share, 32 * tokens), bf16),
+            pltpu.VMEM((2 * share, width), bf16),
+            pltpu.VMEM((share, width), bf16),
+            pltpu.VMEM((32 * tokens, back), bf16),
+            pltpu.VMEM((2, 8 * tokens, back), bf16),
+            pltpu.VMEM((2, 4 * tokens, back), bf16),
+            pltpu.VMEM((4 * tokens, back), bf16),
+            pltpu.VMEM((3, tokens, back), bf16),
+            dma((48,)),
+            dma((32,)),
+            dma((2,)),
+            dma((2,)),
+            dma,
+            dma((3,)),
+            dma((6,)),
+        ],
+        compiler_params=pltpu.CompilerParams(
+            collective_id=0, has_side_effects=True, vmem_limit_bytes=48 * 1024 * 1024
+        ),
+    )(grad_out, x_codes, x_scales, combine, expert_ids, w_gate, w_up, w_down)
+
+
+def chosen_body(grad_out, x_codes, x_scales, combine, expert_ids, w_gate, w_up, w_down):
+    tokens, picks = expert_ids.shape
+    experts = w_gate.shape[0] * lax.axis_size("expert")
+    capacity = min(tokens, max(2, 2 * tokens * picks // experts))
+    sizes = (lax.axis_size("dp"), lax.axis_size("expert"), w_gate.shape[0])
+    chosen = fused_body if capacity == tokens and sizes == (2, 16, 1) else body
+    return chosen(grad_out, x_codes, x_scales, combine, expert_ids, w_gate, w_up, w_down)
+
+
 def solution(mesh):
     in_specs = (
         P(("dp", "expert"), None),
@@ -161,4 +537,4 @@
         P("expert", "dp", None),
         P("expert", "dp", None),
     )
-    return jax.shard_map(body, mesh=mesh, in_specs=in_specs, out_specs=out_specs, check_vma=False)
+    return jax.shard_map(chosen_body, mesh=mesh, in_specs=in_specs, out_specs=out_specs, check_vma=False)

time: 189 us -> 70.1 us (0.37)
  blocking collectives: 89.8 us -> 0 us
  Pallas kernels: 0 us -> 57.8 us
  waiting for transfers between devices: 38.2 us -> 0 us
  matrix products: 19.7 us -> 0 us
  starting transfers between devices: 14.2 us -> 0 us
  between operations: 14 us -> 0.65 us
  other arithmetic: 2.54 us -> 0 us
  local copies, waits for them, and re-layouts: 9.29 us -> 11.3 us
    all_to_all x3 -> x0, blocking collectives: 73.7 us -> none  [the longest x1 32.1 us: body(): lax.all_to_all(code_rows, 'expert', split_axis=0, concat_axis=0, tiled=True)]
    pallas_call x0 -> x1, Pallas kernels: none -> 57.8 us  [fused_body(): pl.pallas_call(functools.partial(expert_kernel, tokens, width, share, lan...]
    all_to_all x3 -> x0, waiting for transfers between devices: 21 us -> none  [the longest x1 13.9 us: body(): lax.all_to_all(summed.reshape(experts, capacity, width).astype(jnp.bfloat...]
    dot_general x11 -> x0, matrix products: 19.7 us -> none  [the longest x1 4.18 us: body(): lax.dot_general(grad_flat, down_w, (((1,), (1,)), ((), ())), preferred_el...]
    reduce_scatter x1 -> x0, waiting for transfers between devices: 14.9 us -> none  [body(): lax.psum_scatter(input_part.reshape(groups, experts, capacity, width).ast...]
    all_to_all x3 -> x0, starting transfers between devices: 14.1 us -> none  [the longest x1 5.63 us: body(): lax.all_to_all(summed.reshape(experts, capacity, width).astype(jnp.bfloat...]
    all_gather x2 -> x0, blocking collectives: 11 us -> none  [the longest x1 6.61 us: body(): lax.all_gather(scale_rows[None], 'dp', axis=0, tiled=True)]
    unnamed x34 -> x14, local copies, waits for them, and re-layouts: 3.57 us -> 10.7 us
  transfers between devices with their start and end apart: 6 -> 0, of which waited for: 5 -> 0; matrix products, arithmetic and copies ran while one was open for 9% -> 0% of each run, Pallas kernels for 0% -> 0%
where the time goes in v2:
time: 70.1 us; the launch traced here: 69.8 us
  Pallas kernels  57.8 us (82%)
  local copies, waits for them, and re-layouts  11.3 us (16%)
    pallas_call x1, Pallas kernels, fused_body(): pl.pallas_call(functools.partial(expert_kernel, tokens, width, share, lan...  57.8 us
    unnamed x14, local copies, waits for them, and re-layouts  10.7 us

profile of v2, /device:TPU:0, one launch (start us, length us, event | category | flops | bytes accessed | tf_op | source)
XLA Modules:
  0.0 69.8 jit_solution(18174086923777418422)
XLA Ops:
  0.6 0.8 %copy.13.combine_ref = bf16[16,8]{1,0:T(8,128)(2,1)S(1)} copy(bf16[16,8]{0,1:T(8,128)(2,1)} %param.11) | data formatting | bytes 512 | tf_op args[3]
  1.4 0.8 %copy.14.ids_ref = s32[16,8]{1,0:T(8,128)S(1)} copy(s32[16,8]{0,1:T(8,128)} %param.12) | data formatting | bytes 1024 | tf_op args[4]
  2.1 0.0 copy-start.1
  2.2 0.8 %copy-done.1 = bf16[16,2048]{1,0:T(8,128)(2,1)S(1)} copy-done((bf16[16,2048]{1,0:T(8,128)(2,1)S(1)}, bf16[16,2048]{1,0:T(8,128)(2,1)}, u32[]{:S(2)}) %copy-start.1) | copy-done | bytes 65560
  3.0 0.0 copy-start.2
  3.0 0.8 %copy-done.2 = bf16[16,2048]{1,0:T(8,128)(2,1)S(1)} copy-done((bf16[16,2048]{1,0:T(8,128)(2,1)S(1)}, bf16[16,2048]{1,0:T(8,128)(2,1)}, u32[]{:S(2)}) %copy-start.2) | copy-done | bytes 65560
  3.8 0.0 copy-start.3
  3.8 0.7 copy-done.3
  4.5 57.8 %shard_map.119 = (bf16[16,2048]{1,0:T(8,128)(2,1)S(1)}, f32[16,8]{1,0:T(8,128)S(1)}, bf16[1,384,2048]{2,1,0:T(8,128)(2,1)S(1)}, bf16[1,384,2048]{2,1,0:T(8,128)(2,1)S(1)}, bf16[1,384,2048]{2,1,0:T(8,128)(2,1)S(1)}) custom-call(bf16[16,2048]{1,0:T(8,128)(2,1)S(1)} %copy-done.1, bf16[16,2048]{1,0:T(8,128)(2,1)S(1)} %copy-done.2, bf16[16,16]{1,0:T(8,128)(2,1)S(1)} %copy-done.3, ...), custom_call_target="tpu_custom_call" | custom-call | tf_op jit(solution)/shard_map/pallas_call | solution.py:471
  62.3 0.0 copy-start
  62.3 1.1 %copy-done = bf16[1,384,2048]{2,1,0:T(8,128)(2,1)} copy-done((bf16[1,384,2048]{2,1,0:T(8,128)(2,1)}, bf16[1,384,2048]{2,1,0:T(8,128)(2,1)S(1)}, u32[]{:S(2)}) %copy-start) | copy-done | bytes 1572888
  63.5 0.7 copy.15
  64.1 0.6 copy.20
  64.8 2.7 %copy.21 = bf16[1,384,2048]{2,1,0:T(8,128)(2,1)} copy(bf16[1,384,2048]{2,1,0:T(8,128)(2,1)} %copy-done) | data formatting | bytes 3145728
  67.5 1.1 %copy.22 = bf16[1,384,2048]{2,1,0:T(8,128)(2,1)} copy(bf16[1,384,2048]{2,1,0:T(8,128)(2,1)S(1)} %get-tuple-element.18) | data formatting | bytes 3145728
  68.6 1.1 %copy.23 = bf16[1,384,2048]{2,1,0:T(8,128)(2,1)} copy(bf16[1,384,2048]{2,1,0:T(8,128)(2,1)S(1)} %get-tuple-element.19) | data formatting | bytes 3145728
Async XLA Ops:
  2.1 0.8 %copy-start.1 = (bf16[16,2048]{1,0:T(8,128)(2,1)S(1)}, bf16[16,2048]{1,0:T(8,128)(2,1)}, u32[]{:S(2)}) copy-start(bf16[16,2048]{1,0:T(8,128)(2,1)} %grad_ref.1) | copy-start | bytes 196612
  3.0 0.8 %copy-start.2 = (bf16[16,2048]{1,0:T(8,128)(2,1)S(1)}, bf16[16,2048]{1,0:T(8,128)(2,1)}, u32[]{:S(2)}) copy-start(bf16[16,2048]{1,0:T(8,128)(2,1)} %codes_ref.1) | copy-start | bytes 196612
  3.8 0.7 copy-start.3
  62.3 1.1 %copy-start = (bf16[1,384,2048]{2,1,0:T(8,128)(2,1)}, bf16[1,384,2048]{2,1,0:T(8,128)(2,1)S(1)}, u32[]{:S(2)}) copy-start(bf16[1,384,2048]{2,1,0:T(8,128)(2,1)S(1)} %get-tuple-element.17) | copy-start | bytes 4718596

commit v3 on v2

--- a/solution.py
+++ b/solution.py
@@ -154,19 +154,22 @@
     share,
     lanes,
     picks,
-    grad_ref,
-    codes_ref,
-    scales_ref,
+    grad_hbm,
+    codes_hbm,
+    scales_hbm,
+    ids_hbm,
     combine_ref,
-    ids_ref,
     gate_hbm,
     up_hbm,
     down_hbm,
     grad_in_ref,
     comb_ref,
-    grad_gate_hbm,
-    grad_up_hbm,
-    grad_down_hbm,
+    grad_gate_ref,
+    grad_up_ref,
+    grad_down_ref,
+    codes_ref,
+    scales_ref,
+    ids_ref,
     rows_buf,
     stack_w,
     down_w,
@@ -176,8 +179,6 @@
     hid_buf,
     act_t,
     hid_t,
-    stack_out,
-    down_out,
     terms,
     from_sib,
     from_first,
@@ -212,7 +213,15 @@
         pltpu.make_async_copy(up_hbm.at[0], stack_w.at[pl.ds(share, share)], local_sems.at[1]),
         pltpu.make_async_copy(down_hbm.at[0], down_w, local_sems.at[2]),
     ]
-    for copy in in_copies:
+    own = z + 4 * (2 * c + other)
+    own_rows = pl.ds(pl.multiple_of(own * tokens, tokens), tokens)
+    own_copies = [
+        pltpu.make_async_copy(codes_hbm, codes_ref, local_sems.at[3]),
+        pltpu.make_async_copy(scales_hbm, scales_ref, local_sems.at[4]),
+        pltpu.make_async_copy(ids_hbm, ids_ref, local_sems.at[5]),
+        pltpu.make_async_copy(grad_hbm, rows_buf.at[own_rows, pl.ds(0, width)], local_sems.at[6]),
+    ]
+    for copy in own_copies + in_copies:
         copy.start()
 
     barrier = pltpu.get_barrier_semaphore()
@@ -225,9 +234,8 @@
     def at_slot(index):
         return pl.ds(pl.multiple_of(index * tokens, tokens), tokens)
 
-    own = slot(0, c, other, z)
-    own_rows = at_slot(own)
-    rows_buf[own_rows, 0:width] = grad_ref[...]
+    for copy in own_copies:
+        copy.wait()
     scales = scales_ref[...].astype(f32)
     for b in range(width // BLOCK):
         cols = slice(b * BLOCK, (b + 1) * BLOCK)
@@ -235,18 +243,25 @@
             codes_ref[:, cols].astype(f32) * scales[:, b : b + 1]
         ).astype(bf16)
     lane = lax.broadcasted_iota(jnp.int32, (tokens, lanes), 1)
+    eye = lax.broadcasted_iota(jnp.int32, (tokens, tokens), 0) == lax.broadcasted_iota(
+        jnp.int32, (tokens, tokens), 1
+    )
+
+    def column(row):
+        return jnp.sum(jnp.where(eye, row, jnp.zeros_like(row)), axis=1, keepdims=True)
+
     combine = combine_ref[...].astype(f32)
-    ids = ids_ref[...]
+    ids = [column(ids_ref[k : k + 1, :]) for k in range(picks)]
     weight_row = jnp.zeros((tokens, lanes), f32)
     for k in range(picks):
-        weight_row += jnp.where(lane == ids[:, k : k + 1], combine[:, k : k + 1], 0.0)
+        weight_row += jnp.where(lane == ids[k], column(combine[k : k + 1, :]), 0.0)
     rows_buf[own_rows, 2 * width :] = weight_row.astype(bf16)
 
     pl.semaphore_wait(barrier, 6)
 
     sent = []
 
-    def send(src, dst, sem, to):
+    def send(src, dst, sem, to, only=None):
         copy = pltpu.make_async_remote_copy(
             src_ref=src,
             dst_ref=dst,
@@ -255,8 +270,11 @@
             device_id=to,
             device_id_type=MESH,
         )
-        copy.start()
-        sent.append(copy)
+        sent.append((copy, only))
+        if only is None:
+            copy.start()
+        else:
+            pl.when(only)(copy.start)
 
     def arrived(ref, sem):
         pltpu.make_async_remote_copy(
@@ -268,21 +286,25 @@
             device_id_type=MESH,
         ).wait_recv()
 
-    def send_rows(src, dst, to):
-        send(rows_buf.at[at_slot(src)], rows_buf.at[at_slot(dst)], row_sems.at[dst], to)
+    def send_rows(src, dst, to, only=None):
+        send(rows_buf.at[at_slot(src)], rows_buf.at[at_slot(dst)], row_sems.at[dst], to, only)
 
     def rows_arrived(index):
         arrived(rows_buf.at[at_slot(index)], row_sems.at[index])
 
-    every_z = [z] + peer_z
+    middle = (z == 1) | (z == 2)
+    near, across = peers[0], peers[2]
+    by_arrival = [peer_z[0], 2 - z // 2, 3 - 3 * (z // 2)]
+    every_z = [z] + by_arrival
+    send_rows(own, own, near)
+    send_rows(own, own, across, middle)
     send_rows(own, own, first)
-    for peer in peers:
-        send_rows(own, own, peer)
     send_rows(own, own + 16, second)
     send_rows(own, own, sib)
-    for pz in peer_z:
+    for pz, onward in zip(by_arrival, (across, near, near)):
         here = slot(0, c, other, pz)
         rows_arrived(here)
+        send_rows(here, here, onward, middle)
         send_rows(here, here, first)
         send_rows(here, here + 16, second)
         send_rows(here, here, sib)
@@ -390,7 +412,7 @@
         def step(i, carry):
             cols = pl.ds(pl.multiple_of(i * tile, tile), tile)
             right = pl.ds(pl.multiple_of(right_start + i * tile, BLOCK), tile)
-            out[:, cols] = jnp.dot(
+            out[0, :, cols] = jnp.dot(
                 left[...], rows_buf[:, right], preferred_element_type=f32
             ).astype(bf16)
             return carry
@@ -412,26 +434,14 @@
     compute(1)
     to_sib(1)
     transpose(1)
-    weight_tiles(hid_t, 0, down_out)
-    out_copies = [pltpu.make_async_copy(down_out, grad_down_hbm.at[0], local_sems.at[3])]
-    out_copies[0].start()
+    weight_tiles(hid_t, 0, grad_down_ref)
     to_first(1)
-    weight_tiles(act_t.at[pl.ds(0, share)], width, stack_out.at[pl.ds(0, share)])
-    out_copies.append(
-        pltpu.make_async_copy(stack_out.at[pl.ds(0, share)], grad_gate_hbm.at[0], local_sems.at[4])
-    )
-    out_copies[1].start()
+    weight_tiles(act_t.at[pl.ds(0, share)], width, grad_gate_ref)
     for half in (1, 0):
         arrived(from_first.at[half], first_sems.at[half])
     add_group(1, other, [from_first.at[1]])
     send(terms.at[group_at(1, other)], from_second, second_sem, second)
-    weight_tiles(act_t.at[pl.ds(share, share)], width, stack_out.at[pl.ds(share, share)])
-    out_copies.append(
-        pltpu.make_async_copy(
-            stack_out.at[pl.ds(share, share)], grad_up_hbm.at[0], local_sems.at[5]
-        )
-    )
-    out_copies[2].start()
+    weight_tiles(act_t.at[pl.ds(share, share)], width, grad_up_ref)
     arrived(from_second, second_sem)
     add_group(0, other, [from_first.at[0], from_second])
     for k in range(3):
@@ -444,18 +454,20 @@
     for k in range(3):
         total += from_z[k].astype(f32)
     grad_in_ref[...] = total[:, 0:width].astype(bf16)
-    place_k = lax.broadcasted_iota(jnp.int32, (tokens, picks), 1)
-    comb_out = jnp.zeros((tokens, picks), f32)
+    place_k = lax.broadcasted_iota(jnp.int32, (picks, tokens), 0)
+    comb_out = jnp.zeros((picks, tokens), f32)
     for k in range(picks):
         value = jnp.sum(
-            jnp.where(lane == ids[:, k : k + 1], total[:, width:], 0.0), axis=1, keepdims=True
-        )
+            jnp.where(lane == ids[k], total[:, width:], 0.0), axis=1, keepdims=True
+        )
+        value = jnp.sum(jnp.where(eye, value, 0.0), axis=0, keepdims=True)
         comb_out += jnp.where(place_k == k, value, 0.0)
     comb_ref[...] = comb_out
-    for copy in sent:
-        copy.wait_send()
-    for copy in out_copies:
-        copy.wait()
+    for copy, only in sent:
+        if only is None:
+            copy.wait_send()
+        else:
+            pl.when(only)(copy.wait_send)
 
 
 def fused_body(grad_out, x_codes, x_scales, combine, expert_ids, w_gate, w_up, w_down):
@@ -466,20 +478,23 @@
     bf16, f32 = jnp.bfloat16, jnp.float32
     back = width + lanes
     vmem = pl.BlockSpec(memory_space=pltpu.VMEM)
-    hbm = pl.BlockSpec(memory_space=pl.ANY)
+    hbm = pl.BlockSpec(memory_space=pltpu.HBM)
     dma = pltpu.SemaphoreType.DMA
-    return pl.pallas_call(
+    outs = pl.pallas_call(
         functools.partial(expert_kernel, tokens, width, share, lanes, picks),
         out_shape=(
             jax.ShapeDtypeStruct(grad_out.shape, bf16),
-            jax.ShapeDtypeStruct(combine.shape, f32),
+            jax.ShapeDtypeStruct((picks, tokens), f32),
             jax.ShapeDtypeStruct(w_gate.shape, bf16),
             jax.ShapeDtypeStruct(w_up.shape, bf16),
             jax.ShapeDtypeStruct(w_down.shape, bf16),
         ),
-        in_specs=[vmem] * 5 + [hbm] * 3,
-        out_specs=(vmem, vmem, hbm, hbm, hbm),
+        in_specs=[hbm] * 4 + [vmem] + [hbm] * 3,
+        out_specs=(vmem,) * 5,
         scratch_shapes=[
+            pltpu.VMEM(x_codes.shape, bf16),
+            pltpu.VMEM(x_scales.shape, bf16),
+            pltpu.VMEM((picks, tokens), jnp.int32),
             pltpu.VMEM((32 * tokens, 2 * width + lanes), bf16),
             pltpu.VMEM((2 * share, width), bf16),
             pltpu.VMEM((share, width), bf16),
@@ -489,25 +504,24 @@
             pltpu.VMEM((16 * tokens, share), bf16),
             pltpu.VMEM((2 * share, 32 * tokens), bf16),
             pltpu.VMEM((share, 32 * tokens), bf16),
-            pltpu.VMEM((2 * share, width), bf16),
-            pltpu.VMEM((share, width), bf16),
             pltpu.VMEM((32 * tokens, back), bf16),
             pltpu.VMEM((2, 8 * tokens, back), bf16),
             pltpu.VMEM((2, 4 * tokens, back), bf16),
             pltpu.VMEM((4 * tokens, back), bf16),
             pltpu.VMEM((3, tokens, back), bf16),
-            dma((48,)),
+            dma((64,)),
             dma((32,)),
             dma((2,)),
             dma((2,)),
             dma,
             dma((3,)),
-            dma((6,)),
+            dma((7,)),
         ],
         compiler_params=pltpu.CompilerParams(
             collective_id=0, has_side_effects=True, vmem_limit_bytes=48 * 1024 * 1024
         ),
-    )(grad_out, x_codes, x_scales, combine, expert_ids, w_gate, w_up, w_down)
+    )(grad_out, x_codes, x_scales, expert_ids.T, combine.T, w_gate, w_up, w_down)
+    return (outs[0], outs[1].T) + tuple(outs[2:])
 
 
 def chosen_body(grad_out, x_codes, x_scales, combine, expert_ids, w_gate, w_up, w_down):

time: 70.1 us -> 65.5 us (0.934)
  local copies, waits for them, and re-layouts: 11.3 us -> 8.38 us
  Pallas kernels: 57.8 us -> 56.2 us
    unnamed x14 -> x15, local copies, waits for them, and re-layouts: 10.7 us -> 8.38 us
    pallas_call x1, Pallas kernels: 57.8 us -> 56.2 us  [fused_body(): pl.pallas_call(functools.partial(expert_kernel, tokens, width, share, lan...]
where the time goes in v3:
time: 65.5 us; the launch traced here: 65.3 us
  Pallas kernels  56.2 us (86%)
  local copies, waits for them, and re-layouts  8.38 us (13%)
  between operations  0.66 us (1%)
    pallas_call x1, Pallas kernels, fused_body(): pl.pallas_call(functools.partial(expert_kernel, tokens, width, share, lan...  56.2 us
    unnamed x15, local copies, waits for them, and re-layouts  8.38 us

profile of v3, /device:TPU:0, one launch (start us, length us, event | category | flops | bytes accessed | tf_op | source)
XLA Modules:
  0.0 65.3 jit_solution(5783213918823592277)
XLA Ops:
  0.6 0.0 copy-start
  0.6 0.8 %copy-done = bf16[16,2048]{1,0:T(8,128)(2,1)S(1)} copy-done((bf16[16,2048]{1,0:T(8,128)(2,1)S(1)}, bf16[16,2048]{1,0:T(8,128)(2,1)}, u32[]{:S(2)}) %copy-start) | copy-done | bytes 65560
  1.5 0.0 copy-start.1
  1.5 0.8 %copy-done.1 = bf16[16,2048]{1,0:T(8,128)(2,1)S(1)} copy-done((bf16[16,2048]{1,0:T(8,128)(2,1)S(1)}, bf16[16,2048]{1,0:T(8,128)(2,1)}, u32[]{:S(2)}) %copy-start.1) | copy-done | bytes 65560
  2.3 0.0 copy-start.2
  2.3 0.7 %copy-done.2 = bf16[16,16]{1,0:T(8,128)(2,1)S(1)} copy-done((bf16[16,16]{1,0:T(8,128)(2,1)S(1)}, bf16[16,16]{1,0:T(8,128)(2,1)}, u32[]{:S(2)}) %copy-start.2) | copy-done | bytes 536
  3.0 0.0 copy-start.3
  3.0 0.7 %copy-done.3 = s32[16,8]{0,1:T(8,128)S(1)} copy-done((s32[16,8]{0,1:T(8,128)S(1)}, s32[16,8]{0,1:T(8,128)}, u32[]{:S(2)}) %copy-start.3) | copy-done | bytes 536
  3.7 0.0 copy-start.4
  3.7 0.7 %copy-done.4 = bf16[16,8]{0,1:T(8,128)(2,1)S(1)} copy-done((bf16[16,8]{0,1:T(8,128)(2,1)S(1)}, bf16[16,8]{0,1:T(8,128)(2,1)}, u32[]{:S(2)}) %copy-start.4) | copy-done | bytes 280
  4.4 56.2 %shard_map.119 = (bf16[16,2048]{1,0:T(8,128)(2,1)S(1)}, f32[8,16]{1,0:T(8,128)S(1)}, bf16[1,384,2048]{2,1,0:T(8,128)(2,1)S(1)}, bf16[1,384,2048]{2,1,0:T(8,128)(2,1)S(1)}, bf16[1,384,2048]{2,1,0:T(8,128)(2,1)S(1)}) custom-call(bf16[16,2048]{1,0:T(8,128)(2,1)S(1)} %copy-done, bf16[16,2048]{1,0:T(8,128)(2,1)S(1)} %copy-done.1, bf16[16,16]{1,0:T(8,128)(2,1)S(1)} %copy-done.2, ...), custom_call_target="tpu_custom_call" | custom-call | tf_op jit(solution)/shard_map/pallas_call | solution.py:483
  60.6 0.6 copy.18
  61.2 0.6 copy.19
  61.8 1.1 %copy.20 = bf16[1,384,2048]{2,1,0:T(8,128)(2,1)} copy(bf16[1,384,2048]{2,1,0:T(8,128)(2,1)S(1)} %get-tuple-element.22) | data formatting | bytes 3145728
  63.0 1.1 %copy.21 = bf16[1,384,2048]{2,1,0:T(8,128)(2,1)} copy(bf16[1,384,2048]{2,1,0:T(8,128)(2,1)S(1)} %get-tuple-element.23) | data formatting | bytes 3145728
  64.1 1.1 %copy.22 = bf16[1,384,2048]{2,1,0:T(8,128)(2,1)} copy(bf16[1,384,2048]{2,1,0:T(8,128)(2,1)S(1)} %get-tuple-element.24) | data formatting | bytes 3145728
Async XLA Ops:
  0.6 0.8 %copy-start = (bf16[16,2048]{1,0:T(8,128)(2,1)S(1)}, bf16[16,2048]{1,0:T(8,128)(2,1)}, u32[]{:S(2)}) copy-start(bf16[16,2048]{1,0:T(8,128)(2,1)} %grad_hbm.1) | copy-start | bytes 196612
  1.5 0.8 %copy-start.1 = (bf16[16,2048]{1,0:T(8,128)(2,1)S(1)}, bf16[16,2048]{1,0:T(8,128)(2,1)}, u32[]{:S(2)}) copy-start(bf16[16,2048]{1,0:T(8,128)(2,1)} %codes_hbm.1) | copy-start | bytes 196612
  2.3 0.7 %copy-start.2 = (bf16[16,16]{1,0:T(8,128)(2,1)S(1)}, bf16[16,16]{1,0:T(8,128)(2,1)}, u32[]{:S(2)}) copy-start(bf16[16,16]{1,0:T(8,128)(2,1)} %scales_hbm.1) | copy-start | bytes 1540
  3.0 0.7 %copy-start.3 = (s32[16,8]{0,1:T(8,128)S(1)}, s32[16,8]{0,1:T(8,128)}, u32[]{:S(2)}) copy-start(s32[16,8]{0,1:T(8,128)} %param.12) | copy-start | bytes 1540
  3.7 0.7 %copy-start.4 = (bf16[16,8]{0,1:T(8,128)(2,1)S(1)}, bf16[16,8]{0,1:T(8,128)(2,1)}, u32[]{:S(2)}) copy-start(bf16[16,8]{0,1:T(8,128)(2,1)} %param.11) | copy-start | bytes 772

commit v4 on v3

--- a/solution.py
+++ b/solution.py
@@ -158,18 +158,19 @@
     codes_hbm,
     scales_hbm,
     ids_hbm,
-    combine_ref,
+    combine_hbm,
     gate_hbm,
     up_hbm,
     down_hbm,
     grad_in_ref,
     comb_ref,
-    grad_gate_ref,
-    grad_up_ref,
-    grad_down_ref,
+    grad_gate_hbm,
+    grad_up_hbm,
+    grad_down_hbm,
     codes_ref,
     scales_ref,
     ids_ref,
+    combine_ref,
     rows_buf,
     stack_w,
     down_w,
@@ -179,6 +180,8 @@
     hid_buf,
     act_t,
     hid_t,
+    stack_out,
+    down_out,
     terms,
     from_sib,
     from_first,
@@ -188,7 +191,7 @@
     row_sems,
     sib_sems,
     first_sems,
-    second_sem,
+    second_sems,
     z_sems,
     local_sems,
 ):
@@ -219,6 +222,7 @@
         pltpu.make_async_copy(codes_hbm, codes_ref, local_sems.at[3]),
         pltpu.make_async_copy(scales_hbm, scales_ref, local_sems.at[4]),
         pltpu.make_async_copy(ids_hbm, ids_ref, local_sems.at[5]),
+        pltpu.make_async_copy(combine_hbm, combine_ref, local_sems.at[7]),
         pltpu.make_async_copy(grad_hbm, rows_buf.at[own_rows, pl.ds(0, width)], local_sems.at[6]),
     ]
     for copy in own_copies + in_copies:
@@ -323,6 +327,11 @@
     strip = 2 * tokens
     mine = lax.broadcasted_iota(jnp.int32, (strip, lanes), 1) == place
 
+    parts = ((0, width // 2), (width // 2, width // 2 + lanes))
+
+    def part(h):
+        return pl.ds(*parts[h])
+
     def compute(half):
         base = half * half_rows
         grad_rows = rows_buf[base : base + half_rows, 0:width]
@@ -368,7 +377,11 @@
             ).astype(bf16)
             return carry
 
-        lax.fori_loop(0, width // tile, back_tile, 0)
+        tiles = width // tile
+        lax.fori_loop(0, tiles // 2, back_tile, 0)
+        to_sib(half, 0)
+        lax.fori_loop(tiles // 2, tiles, back_tile, 0)
+        to_sib(half, 1)
 
     def fam_at(half, fam):
         return pl.ds(pl.multiple_of(half * half_rows + fam * fam_rows, fam_rows), fam_rows)
@@ -379,86 +392,133 @@
             group_rows,
         )
 
-    def to_sib(half):
-        send(terms.at[fam_at(half, 1 - c)], from_sib.at[half], sib_sems.at[half], sib)
-
-    def transpose(half):
-        cols = slice(half * half_rows, (half + 1) * half_rows)
-        act_t[:, cols] = act_buf[...].T
-        hid_t[:, cols] = hid_buf[...].T
-
-    def add_group(half, oth, others):
+    def to_sib(half, h):
+        send(
+            terms.at[fam_at(half, 1 - c), part(h)],
+            from_sib.at[half, :, part(h)],
+            sib_sems.at[2 * half + h],
+            sib,
+        )
+
+    def transpose(half, source, target):
+        target[:, half * half_rows : (half + 1) * half_rows] = source[...].T
+
+    def add_group(half, oth, h, others):
+        cols = part(h)
+
         def add(i, carry):
             at = half * half_rows + c * fam_rows + oth * group_rows + i * tokens
             at = pl.ds(pl.multiple_of(at, tokens), tokens)
             sib_at = pl.ds(pl.multiple_of(oth * group_rows + i * tokens, tokens), tokens)
             rest = pl.ds(pl.multiple_of(i * tokens, tokens), tokens)
-            total = terms[at, :].astype(f32) + from_sib[half, sib_at, :].astype(f32)
+            total = terms[at, cols].astype(f32) + from_sib[half, sib_at, cols].astype(f32)
             for ref in others:
-                total += ref[rest, :].astype(f32)
-            terms[at, :] = total.astype(bf16)
+                total += ref[rest, cols].astype(f32)
+            terms[at, cols] = total.astype(bf16)
             return carry
 
         lax.fori_loop(0, 4, add, 0)
 
-    def to_first(half):
-        arrived(from_sib.at[half], sib_sems.at[half])
-        add_group(half, 1 - other, [])
-        send(terms.at[group_at(half, 1 - other)], from_first.at[half], first_sems.at[half], first)
-
-    def weight_tiles(left, right_start, out):
+    def to_first(half, h):
+        arrived(from_sib.at[half, :, part(h)], sib_sems.at[2 * half + h])
+        add_group(half, 1 - other, h, [])
+        send(
+            terms.at[group_at(half, 1 - other), part(h)],
+            from_first.at[half, :, part(h)],
+            first_sems.at[2 * half + h],
+            first,
+        )
+
+    def to_second(h):
+        arrived(from_first.at[1, :, part(h)], first_sems.at[2 + h])
+        add_group(1, other, h, [from_first.at[1]])
+        send(
+            terms.at[group_at(1, other), part(h)],
+            from_second.at[:, part(h)],
+            second_sems.at[h],
+            second,
+        )
+
+    def to_z(h):
+        arrived(from_first.at[0, :, part(h)], first_sems.at[h])
+        arrived(from_second.at[:, part(h)], second_sems.at[h])
+        add_group(0, other, h, [from_first.at[0], from_second])
+        for k in range(3):
+            send(
+                terms.at[at_slot(slot(0, c, other, peer_z[k])), part(h)],
+                from_z.at[k, :, part(h)],
+                z_sems.at[3 * h + k],
+                peers[k],
+            )
+
+    def summed(h):
+        total = terms[own_rows, part(h)].astype(f32)
+        for k in range(3):
+            arrived(from_z.at[k, :, part(h)], z_sems.at[3 * h + k])
+        for k in range(3):
+            total += from_z[k, :, part(h)].astype(f32)
+        return total
+
+    def weight_tiles(left, right_start, out, begin, end):
         tile = 512
 
         def step(i, carry):
             cols = pl.ds(pl.multiple_of(i * tile, tile), tile)
             right = pl.ds(pl.multiple_of(right_start + i * tile, BLOCK), tile)
-            out[0, :, cols] = jnp.dot(
+            out[:, cols] = jnp.dot(
                 left[...], rows_buf[:, right], preferred_element_type=f32
             ).astype(bf16)
             return carry
 
-        lax.fori_loop(0, width // tile, step, 0)
+        lax.fori_loop(begin, end, step, 0)
 
     compute(0)
-    to_sib(0)
-    transpose(0)
+    transpose(0, hid_buf, hid_t)
+    transpose(0, act_buf, act_t)
     for oth in (other, 1 - other):
         for pz in every_z:
             here = slot(1, c, oth, pz)
             rows_arrived(here)
             send_rows(here, here, sib)
-    to_first(0)
+    to_first(0, 0)
+    to_first(0, 1)
     for oth in (other, 1 - other):
         for pz in every_z:
             rows_arrived(slot(1, 1 - c, oth, pz))
     compute(1)
-    to_sib(1)
-    transpose(1)
-    weight_tiles(hid_t, 0, grad_down_ref)
-    to_first(1)
-    weight_tiles(act_t.at[pl.ds(0, share)], width, grad_gate_ref)
-    for half in (1, 0):
-        arrived(from_first.at[half], first_sems.at[half])
-    add_group(1, other, [from_first.at[1]])
-    send(terms.at[group_at(1, other)], from_second, second_sem, second)
-    weight_tiles(act_t.at[pl.ds(share, share)], width, grad_up_ref)
-    arrived(from_second, second_sem)
-    add_group(0, other, [from_first.at[0], from_second])
-    for k in range(3):
-        send(
-            terms.at[at_slot(slot(0, c, other, peer_z[k]))], from_z.at[k], z_sems.at[k], peers[k]
-        )
-    for k in range(3):
-        arrived(from_z.at[k], z_sems.at[k])
-    total = terms[own_rows, :].astype(f32)
-    for k in range(3):
-        total += from_z[k].astype(f32)
-    grad_in_ref[...] = total[:, 0:width].astype(bf16)
+    tiles = width // 512
+    gate_at, up_at = pl.ds(0, share), pl.ds(share, share)
+    out_copies = [
+        pltpu.make_async_copy(down_out, grad_down_hbm.at[0], local_sems.at[8]),
+        pltpu.make_async_copy(stack_out.at[gate_at], grad_gate_hbm.at[0], local_sems.at[9]),
+        pltpu.make_async_copy(stack_out.at[up_at], grad_up_hbm.at[0], local_sems.at[10]),
+    ]
+    transpose(1, hid_buf, hid_t)
+    weight_tiles(hid_t, 0, down_out, 0, tiles // 2)
+    to_first(1, 0)
+    weight_tiles(hid_t, 0, down_out, tiles // 2, tiles)
+    out_copies[0].start()
+    to_first(1, 1)
+    transpose(1, act_buf, act_t)
+    weight_tiles(act_t.at[gate_at], width, stack_out.at[gate_at], 0, tiles)
+    out_copies[1].start()
+    to_second(0)
+    weight_tiles(act_t.at[up_at], width, stack_out.at[up_at], 0, tiles // 2)
+    to_second(1)
+    weight_tiles(act_t.at[up_at], width, stack_out.at[up_at], tiles // 2, tiles)
+    out_copies[2].start()
+    to_z(0)
+    to_z(1)
+    total = summed(0)
+    grad_in_ref[:, 0 : width // 2] = total.astype(bf16)
+    total = summed(1)
+    grad_in_ref[:, width // 2 :] = total[:, 0 : width // 2].astype(bf16)
+    comb_total = total[:, width // 2 :]
     place_k = lax.broadcasted_iota(jnp.int32, (picks, tokens), 0)
     comb_out = jnp.zeros((picks, tokens), f32)
     for k in range(picks):
         value = jnp.sum(
-            jnp.where(lane == ids[k], total[:, width:], 0.0), axis=1, keepdims=True
+            jnp.where(lane == ids[k], comb_total, 0.0), axis=1, keepdims=True
         )
         value = jnp.sum(jnp.where(eye, value, 0.0), axis=0, keepdims=True)
         comb_out += jnp.where(place_k == k, value, 0.0)
@@ -468,6 +528,8 @@
             copy.wait_send()
         else:
             pl.when(only)(copy.wait_send)
+    for copy in out_copies:
+        copy.wait()
 
 
 def fused_body(grad_out, x_codes, x_scales, combine, expert_ids, w_gate, w_up, w_down):
@@ -489,12 +551,13 @@
             jax.ShapeDtypeStruct(w_up.shape, bf16),
             jax.ShapeDtypeStruct(w_down.shape, bf16),
         ),
-        in_specs=[hbm] * 4 + [vmem] + [hbm] * 3,
-        out_specs=(vmem,) * 5,
+        in_specs=[hbm] * 8,
+        out_specs=(vmem, vmem, hbm, hbm, hbm),
         scratch_shapes=[
             pltpu.VMEM(x_codes.shape, bf16),
             pltpu.VMEM(x_scales.shape, bf16),
             pltpu.VMEM((picks, tokens), jnp.int32),
+            pltpu.VMEM((picks, tokens), bf16),
             pltpu.VMEM((32 * tokens, 2 * width + lanes), bf16),
             pltpu.VMEM((2 * share, width), bf16),
             pltpu.VMEM((share, width), bf16),
@@ -504,6 +567,8 @@
             pltpu.VMEM((16 * tokens, share), bf16),
             pltpu.VMEM((2 * share, 32 * tokens), bf16),
             pltpu.VMEM((share, 32 * tokens), bf16),
+            pltpu.VMEM((2 * share, width), bf16),
+            pltpu.VMEM((share, width), bf16),
             pltpu.VMEM((32 * tokens, back), bf16),
             pltpu.VMEM((2, 8 * tokens, back), bf16),
             pltpu.VMEM((2, 4 * tokens, back), bf16),
@@ -511,14 +576,14 @@
             pltpu.VMEM((3, tokens, back), bf16),
             dma((64,)),
             dma((32,)),
+            dma((4,)),
+            dma((4,)),
             dma((2,)),
-            dma((2,)),
-            dma,
-            dma((3,)),
-            dma((7,)),
+            dma((6,)),
+            dma((11,)),
         ],
         compiler_params=pltpu.CompilerParams(
-            collective_id=0, has_side_effects=True, vmem_limit_bytes=48 * 1024 * 1024
+            collective_id=0, has_side_effects=True, vmem_limit_bytes=56 * 1024 * 1024
         ),
     )(grad_out, x_codes, x_scales, expert_ids.T, combine.T, w_gate, w_up, w_down)
     return (outs[0], outs[1].T) + tuple(outs[2:])

time: 65.5 us -> 63 us (0.962)
  Pallas kernels: 56.2 us -> 53.4 us
    pallas_call x1, Pallas kernels: 56.2 us -> 53.4 us  [fused_body(): pl.pallas_call(functools.partial(expert_kernel, tokens, width, share, lan...]
    unnamed x15 -> x9, local copies, waits for them, and re-layouts: 8.38 us -> 8.72 us
where the time goes in v4:
time: 63 us; the launch traced here: 62.8 us
  Pallas kernels  53.4 us (85%)
  local copies, waits for them, and re-layouts  8.72 us (14%)
  between operations  0.65 us (1%)
    pallas_call x1, Pallas kernels, fused_body(): pl.pallas_call(functools.partial(expert_kernel, tokens, width, share, lan...  53.4 us
    unnamed x9, local copies, waits for them, and re-layouts  8.72 us

profile of v4, /device:TPU:0, one launch (start us, length us, event | category | flops | bytes accessed | tf_op | source)
XLA Modules:
  0.0 62.8 jit_solution(9888282795719189349)
XLA Ops:
  0.6 53.4 %shard_map.119 = (bf16[16,2048]{1,0:T(8,128)(2,1)}, f32[8,16]{1,0:T(8,128)}, bf16[1,384,2048]{2,1,0:T(8,128)(2,1)}, bf16[1,384,2048]{2,1,0:T(8,128)(2,1)}, bf16[1,384,2048]{2,1,0:T(8,128)(2,1)}) custom-call(bf16[16,2048]{1,0:T(8,128)(2,1)} %grad_hbm.1, bf16[16,2048]{1,0:T(8,128)(2,1)} %codes_hbm.1, bf16[16,16]{1,0:T(8,128)(2,1)} %scales_hbm.1, ...), custom_call_target="tpu_custom_call" | custom-call | tf_op jit(solution)/shard_map/pallas_call | solution.py:545
  54.0 1.5 %copy.18 = bf16[16,2048]{1,0:T(8,128)(2,1)} copy(bf16[16,2048]{1,0:T(8,128)(2,1)} %get-tuple-element.20) | data formatting | bytes 131072
  55.5 1.3 %copy.19 = f32[16,8]{0,1:T(8,128)} copy(f32[16,8]{0,1:T(8,128)} %bitcast.3) | data formatting | bytes 1024
  56.8 0.0 copy-start.1
  56.8 2.8 %copy.20 = bf16[1,384,2048]{2,1,0:T(8,128)(2,1)} copy(bf16[1,384,2048]{2,1,0:T(8,128)(2,1)} %get-tuple-element.22) | data formatting | bytes 3145728
  59.6 0.0 copy-done.1
  59.6 0.0 copy-start
  59.7 1.1 %copy.21 = bf16[1,384,2048]{2,1,0:T(8,128)(2,1)} copy(bf16[1,384,2048]{2,1,0:T(8,128)(2,1)S(1)} %copy-done.1) | data formatting | bytes 3145728
  60.8 0.8 %copy-done = bf16[1,384,2048]{2,1,0:T(8,128)(2,1)S(1)} copy-done((bf16[1,384,2048]{2,1,0:T(8,128)(2,1)S(1)}, bf16[1,384,2048]{2,1,0:T(8,128)(2,1)}, u32[]{:S(2)}) %copy-start) | copy-done | bytes 1572888
  61.6 1.1 %copy.22 = bf16[1,384,2048]{2,1,0:T(8,128)(2,1)} copy(bf16[1,384,2048]{2,1,0:T(8,128)(2,1)S(1)} %copy-done) | data formatting | bytes 3145728
Async XLA Ops:
  56.8 2.9 %copy-start.1 = (bf16[1,384,2048]{2,1,0:T(8,128)(2,1)S(1)}, bf16[1,384,2048]{2,1,0:T(8,128)(2,1)}, u32[]{:S(2)}) copy-start(bf16[1,384,2048]{2,1,0:T(8,128)(2,1)} %get-tuple-element.23) | copy-start | bytes 4718596
  59.6 2.0 %copy-start = (bf16[1,384,2048]{2,1,0:T(8,128)(2,1)S(1)}, bf16[1,384,2048]{2,1,0:T(8,128)(2,1)}, u32[]{:S(2)}) copy-start(bf16[1,384,2048]{2,1,0:T(8,128)(2,1)} %get-tuple-element.24) | copy-start | bytes 4718596

commit v5 on v4

--- a/solution.py
+++ b/solution.py
@@ -290,36 +290,48 @@
             device_id_type=MESH,
         ).wait_recv()
 
-    def send_rows(src, dst, to, only=None):
-        send(rows_buf.at[at_slot(src)], rows_buf.at[at_slot(dst)], row_sems.at[dst], to, only)
-
-    def rows_arrived(index):
-        arrived(rows_buf.at[at_slot(index)], row_sems.at[index])
+    row_parts = (pl.ds(0, width), pl.ds(width, width + lanes))
+
+    def send_rows(q, src, dst, to, only=None):
+        send(
+            rows_buf.at[at_slot(src), row_parts[q]],
+            rows_buf.at[at_slot(dst), row_parts[q]],
+            row_sems.at[q, dst],
+            to,
+            only,
+        )
+
+    def rows_arrived(q, index):
+        arrived(rows_buf.at[at_slot(index), row_parts[q]], row_sems.at[q, index])
 
     middle = (z == 1) | (z == 2)
     near, across = peers[0], peers[2]
     by_arrival = [peer_z[0], 2 - z // 2, 3 - 3 * (z // 2)]
     every_z = [z] + by_arrival
-    send_rows(own, own, near)
-    send_rows(own, own, across, middle)
-    send_rows(own, own, first)
-    send_rows(own, own + 16, second)
-    send_rows(own, own, sib)
+    for q in range(2):
+        send_rows(q, own, own, near)
+        send_rows(q, own, own, across, middle)
+        send_rows(q, own, own, first)
+        send_rows(q, own, own + 16, second)
+        send_rows(q, own, own, sib)
     for pz, onward in zip(by_arrival, (across, near, near)):
         here = slot(0, c, other, pz)
-        rows_arrived(here)
-        send_rows(here, here, onward, middle)
-        send_rows(here, here, first)
-        send_rows(here, here + 16, second)
-        send_rows(here, here, sib)
+        for q in range(2):
+            rows_arrived(q, here)
+            send_rows(q, here, here, onward, middle)
+            send_rows(q, here, here, first)
+            send_rows(q, here, here + 16, second)
+            send_rows(q, here, here, sib)
     for pz in every_z:
         here = slot(0, c, 1 - other, pz)
-        rows_arrived(here)
-        send_rows(here, here + 16, second)
-        send_rows(here, here, sib)
+        for q in range(2):
+            rows_arrived(q, here)
+            send_rows(q, here, here + 16, second)
+            send_rows(q, here, here, sib)
     for oth in (other, 1 - other):
         for pz in every_z:
-            rows_arrived(slot(0, 1 - c, oth, pz))
+            for q in range(2):
+                rows_arrived(q, slot(0, 1 - c, oth, pz))
     for copy in in_copies:
         copy.wait()
 
@@ -478,13 +490,15 @@
     for oth in (other, 1 - other):
         for pz in every_z:
             here = slot(1, c, oth, pz)
-            rows_arrived(here)
-            send_rows(here, here, sib)
+            for q in range(2):
+                rows_arrived(q, here)
+                send_rows(q, here, here, sib)
     to_first(0, 0)
     to_first(0, 1)
     for oth in (other, 1 - other):
         for pz in every_z:
-            rows_arrived(slot(1, 1 - c, oth, pz))
+            for q in range(2):
+                rows_arrived(q, slot(1, 1 - c, oth, pz))
     compute(1)
     tiles = width // 512
     gate_at, up_at = pl.ds(0, share), pl.ds(share, share)
@@ -529,6 +543,15 @@
         else:
             pl.when(only)(copy.wait_send)
     for copy in out_copies:
+        copy.wait()
+
+
+def deliver_kernel(*refs):
+    sems = refs[10]
+    copies = [pltpu.make_async_copy(refs[i], refs[5 + i], sems.at[i]) for i in range(5)]
+    for copy in copies:
+        copy.start()
+    for copy in copies:
         copy.wait()
 
 
@@ -574,8 +597,8 @@
             pltpu.VMEM((2, 4 * tokens, back), bf16),
             pltpu.VMEM((4 * tokens, back), bf16),
             pltpu.VMEM((3, tokens, back), bf16),
-            dma((64,)),
-            dma((32,)),
+            dma((96,)),
+            dma((2, 32)),
             dma((4,)),
             dma((4,)),
             dma((2,)),
@@ -586,6 +609,14 @@
             collective_id=0, has_side_effects=True, vmem_limit_bytes=56 * 1024 * 1024
         ),
     )(grad_out, x_codes, x_scales, expert_ids.T, combine.T, w_gate, w_up, w_down)
+    outs = pl.pallas_call(
+        deliver_kernel,
+        out_shape=tuple(jax.ShapeDtypeStruct(out.shape, out.dtype) for out in outs),
+        in_specs=[hbm] * 5,
+        out_specs=(hbm,) * 5,
+        scratch_shapes=[dma((5,))],
+        compiler_params=pltpu.CompilerParams(vmem_limit_bytes=56 * 1024 * 1024),
+    )(*outs)
     return (outs[0], outs[1].T) + tuple(outs[2:])
 
 

time: 63 us -> 199 us (3.16)
  Pallas kernels: 53.4 us -> 198 us
  local copies, waits for them, and re-layouts: 8.72 us -> 0 us
    pallas_call x0 -> x1, Pallas kernels: none -> 146 us  [fused_body(): pl.pallas_call(deliver_kernel, out_shape=tuple((jax.ShapeDtypeStruct(out....]
    unnamed x9 -> x0, local copies, waits for them, and re-layouts: 8.72 us -> none
where the time goes in v5:
time: 199 us
  Pallas kernels  198 us (99%)
    pallas_call x1, Pallas kernels, fused_body(): pl.pallas_call(deliver_kernel, out_shape=tuple((jax.ShapeDtypeStruct(out....  146 us
    pallas_call x1, Pallas kernels, fused_body(): pl.pallas_call(functools.partial(expert_kernel, tokens, width, share, lan...  52.2 us

profile of v5, /device:TPU:0, one launch (start us, length us, event | category | flops | bytes accessed | tf_op | source)
XLA Modules:
  0.0 199.0 jit_solution(4601360342055186096)
XLA Ops:
  0.6 52.2 %shard_map.119 = (bf16[16,2048]{1,0:T(8,128)(2,1)}, f32[8,16]{1,0:T(8,128)}, bf16[1,384,2048]{2,1,0:T(8,128)(2,1)}, bf16[1,384,2048]{2,1,0:T(8,128)(2,1)}, bf16[1,384,2048]{2,1,0:T(8,128)(2,1)}) custom-call(bf16[16,2048]{1,0:T(8,128)(2,1)} %grad_hbm.1, bf16[16,2048]{1,0:T(8,128)(2,1)} %codes_hbm.1, bf16[16,16]{1,0:T(8,128)(2,1)} %scales_hbm.1, ...), custom_call_target="tpu_custom_call" | custom-call | tf_op jit(solution)/shard_map/pallas_call | solution.py:568
  52.8 146.2 %shard_map.120 = (bf16[16,2048]{1,0:T(8,128)(2,1)}, f32[8,16]{1,0:T(8,128)}, bf16[1,384,2048]{2,1,0:T(8,128)(2,1)}, bf16[1,384,2048]{2,1,0:T(8,128)(2,1)}, bf16[1,384,2048]{2,1,0:T(8,128)(2,1)}) custom-call(bf16[16,2048]{1,0:T(8,128)(2,1)} %get-tuple-element.15.refs_0_, f32[8,16]{1,0:T(8,128)} %get-tuple-element.16.refs_1_, ...), custom_call_target="tpu_custom_call" | custom-call | tf_op jit(solution)/shard_map/pallas_call | solution.py:612

commit v6 on v5

--- a/solution.py
+++ b/solution.py
@@ -182,6 +182,8 @@
     hid_t,
     stack_out,
     down_out,
+    stack_acc,
+    down_acc,
     terms,
     from_sib,
     from_first,
@@ -471,55 +473,74 @@
             total += from_z[k, :, part(h)].astype(f32)
         return total
 
-    def weight_tiles(left, right_start, out, begin, end):
+    def weight_tiles(half, left, right_start, acc, out, begin, end):
         tile = 512
+        taken = slice(half * half_rows, (half + 1) * half_rows)
 
         def step(i, carry):
             cols = pl.ds(pl.multiple_of(i * tile, tile), tile)
             right = pl.ds(pl.multiple_of(right_start + i * tile, BLOCK), tile)
-            out[:, cols] = jnp.dot(
-                left[...], rows_buf[:, right], preferred_element_type=f32
-            ).astype(bf16)
+            product = jnp.dot(left[:, taken], rows_buf[taken, right], preferred_element_type=f32)
+            if half == 0:
+                acc[:, cols] = product
+            else:
+                out[:, cols] = (acc[:, cols] + product).astype(bf16)
             return carry
 
         lax.fori_loop(begin, end, step, 0)
+
+    tiles = width // 512
+    gate_at, up_at = pl.ds(0, share), pl.ds(share, share)
+
+    def down_tiles(half, begin, end):
+        weight_tiles(half, hid_t, 0, down_acc, down_out, begin, end)
+
+    def stack_tiles(half, at, begin, end):
+        weight_tiles(
+            half, act_t.at[at], width, stack_acc.at[at], stack_out.at[at], begin, end
+        )
 
     compute(0)
     transpose(0, hid_buf, hid_t)
     transpose(0, act_buf, act_t)
-    for oth in (other, 1 - other):
+    to_first(0, 0)
+    to_first(0, 1)
+
+    def pass_on(oth):
         for pz in every_z:
             here = slot(1, c, oth, pz)
             for q in range(2):
                 rows_arrived(q, here)
                 send_rows(q, here, here, sib)
-    to_first(0, 0)
-    to_first(0, 1)
+
+    down_tiles(0, 0, tiles)
+    pass_on(other)
+    stack_tiles(0, gate_at, 0, tiles)
+    stack_tiles(0, up_at, 0, tiles)
+    pass_on(1 - other)
     for oth in (other, 1 - other):
         for pz in every_z:
             for q in range(2):
                 rows_arrived(q, slot(1, 1 - c, oth, pz))
     compute(1)
-    tiles = width // 512
-    gate_at, up_at = pl.ds(0, share), pl.ds(share, share)
     out_copies = [
         pltpu.make_async_copy(down_out, grad_down_hbm.at[0], local_sems.at[8]),
         pltpu.make_async_copy(stack_out.at[gate_at], grad_gate_hbm.at[0], local_sems.at[9]),
         pltpu.make_async_copy(stack_out.at[up_at], grad_up_hbm.at[0], local_sems.at[10]),
     ]
     transpose(1, hid_buf, hid_t)
-    weight_tiles(hid_t, 0, down_out, 0, tiles // 2)
+    down_tiles(1, 0, tiles // 2)
     to_first(1, 0)
-    weight_tiles(hid_t, 0, down_out, tiles // 2, tiles)
+    down_tiles(1, tiles // 2, tiles)
     out_copies[0].start()
     to_first(1, 1)
     transpose(1, act_buf, act_t)
-    weight_tiles(act_t.at[gate_at], width, stack_out.at[gate_at], 0, tiles)
+    stack_tiles(1, gate_at, 0, tiles)
     out_copies[1].start()
     to_second(0)
-    weight_tiles(act_t.at[up_at], width, stack_out.at[up_at], 0, tiles // 2)
+    stack_tiles(1, up_at, 0, tiles // 2)
     to_second(1)
-    weight_tiles(act_t.at[up_at], width, stack_out.at[up_at], tiles // 2, tiles)
+    stack_tiles(1, up_at, tiles // 2, tiles)
     out_copies[2].start()
     to_z(0)
     to_z(1)
@@ -547,11 +568,28 @@
 
 
 def deliver_kernel(*refs):
-    sems = refs[10]
-    copies = [pltpu.make_async_copy(refs[i], refs[5 + i], sems.at[i]) for i in range(5)]
-    for copy in copies:
+    sources, results, held, sems = refs[:5], refs[5:10], refs[10:15], refs[15]
+    pieces = []
+    for i in range(5):
+        if len(sources[i].shape) == 3:
+            step = sources[i].shape[1] // 4
+            for j in range(4):
+                at = pl.ds(j * step, step)
+                pieces.append((sources[i].at[0, at], held[i].at[0, at], results[i].at[0, at]))
+        else:
+            pieces.append((sources[i], held[i], results[i]))
+    reads = [
+        pltpu.make_async_copy(piece[0], piece[1], sems.at[0, n]) for n, piece in enumerate(pieces)
+    ]
+    writes = [
+        pltpu.make_async_copy(piece[1], piece[2], sems.at[1, n]) for n, piece in enumerate(pieces)
+    ]
+    for copy in reads:
         copy.start()
-    for copy in copies:
+    for n in range(len(pieces)):
+        reads[n].wait()
+        writes[n].start()
+    for copy in writes:
         copy.wait()
 
 
@@ -592,6 +630,8 @@
             pltpu.VMEM((share, 32 * tokens), bf16),
             pltpu.VMEM((2 * share, width), bf16),
             pltpu.VMEM((share, width), bf16),
+            pltpu.VMEM((2 * share, width), f32),
+            pltpu.VMEM((share, width), f32),
             pltpu.VMEM((32 * tokens, back), bf16),
             pltpu.VMEM((2, 8 * tokens, back), bf16),
             pltpu.VMEM((2, 4 * tokens, back), bf16),
@@ -614,7 +654,7 @@
         out_shape=tuple(jax.ShapeDtypeStruct(out.shape, out.dtype) for out in outs),
         in_specs=[hbm] * 5,
         out_specs=(hbm,) * 5,
-        scratch_shapes=[dma((5,))],
+        scratch_shapes=[pltpu.VMEM(out.shape, out.dtype) for out in outs] + [dma((2, 14))],
         compiler_params=pltpu.CompilerParams(vmem_limit_bytes=56 * 1024 * 1024),
     )(*outs)
     return (outs[0], outs[1].T) + tuple(outs[2:])

time: 199 us -> 60 us (0.30)
  Pallas kernels: 198 us -> 59.2 us
    pallas_call x1, Pallas kernels: 146 us -> 4.42 us  [fused_body(): pl.pallas_call(deliver_kernel, out_shape=tuple((jax.ShapeDtypeStruct(out....]
    pallas_call x1, Pallas kernels: 52.2 us -> 54.8 us  [fused_body(): pl.pallas_call(functools.partial(expert_kernel, tokens, width, share, lan...]
where the time goes in v6:
time: 60 us; the launch traced here: 59.9 us
  Pallas kernels  59.2 us (99%)
  between operations  0.64 us (1%)
    pallas_call x1, Pallas kernels, fused_body(): pl.pallas_call(functools.partial(expert_kernel, tokens, width, share, lan...  54.8 us
    pallas_call x1, Pallas kernels, fused_body(): pl.pallas_call(deliver_kernel, out_shape=tuple((jax.ShapeDtypeStruct(out....  4.42 us

profile of v6, /device:TPU:0, one launch (start us, length us, event | category | flops | bytes accessed | tf_op | source)
XLA Modules:
  0.0 59.9 jit_solution(6850596726932488763)
XLA Ops:
  0.6 54.8 %shard_map.119 = (bf16[16,2048]{1,0:T(8,128)(2,1)}, f32[8,16]{1,0:T(8,128)}, bf16[1,384,2048]{2,1,0:T(8,128)(2,1)}, bf16[1,384,2048]{2,1,0:T(8,128)(2,1)}, bf16[1,384,2048]{2,1,0:T(8,128)(2,1)}) custom-call(bf16[16,2048]{1,0:T(8,128)(2,1)} %grad_hbm.1, bf16[16,2048]{1,0:T(8,128)(2,1)} %codes_hbm.1, bf16[16,16]{1,0:T(8,128)(2,1)} %scales_hbm.1, ...), custom_call_target="tpu_custom_call" | custom-call | tf_op jit(solution)/shard_map/pallas_call | solution.py:606
  55.5 4.4 %shard_map.120 = (bf16[16,2048]{1,0:T(8,128)(2,1)}, f32[8,16]{1,0:T(8,128)}, bf16[1,384,2048]{2,1,0:T(8,128)(2,1)}, bf16[1,384,2048]{2,1,0:T(8,128)(2,1)}, bf16[1,384,2048]{2,1,0:T(8,128)(2,1)}) custom-call(bf16[16,2048]{1,0:T(8,128)(2,1)} %get-tuple-element.15.refs_0_, f32[8,16]{1,0:T(8,128)} %get-tuple-element.16.refs_1_, ...), custom_call_target="tpu_custom_call" | custom-call | tf_op jit(solution)/shard_map/pallas_call | solution.py:652

commit v7 on v5

--- a/solution.py
+++ b/solution.py
@@ -547,11 +547,28 @@
 
 
 def deliver_kernel(*refs):
-    sems = refs[10]
-    copies = [pltpu.make_async_copy(refs[i], refs[5 + i], sems.at[i]) for i in range(5)]
-    for copy in copies:
+    sources, results, held, sems = refs[:5], refs[5:10], refs[10:15], refs[15]
+    pieces = []
+    for i in range(5):
+        if len(sources[i].shape) == 3:
+            step = sources[i].shape[1] // 4
+            for j in range(4):
+                at = pl.ds(j * step, step)
+                pieces.append((sources[i].at[0, at], held[i].at[0, at], results[i].at[0, at]))
+        else:
+            pieces.append((sources[i], held[i], results[i]))
+    reads = [
+        pltpu.make_async_copy(piece[0], piece[1], sems.at[0, n]) for n, piece in enumerate(pieces)
+    ]
+    writes = [
+        pltpu.make_async_copy(piece[1], piece[2], sems.at[1, n]) for n, piece in enumerate(pieces)
+    ]
+    for copy in reads:
         copy.start()
-    for copy in copies:
+    for n in range(len(pieces)):
+        reads[n].wait()
+        writes[n].start()
+    for copy in writes:
         copy.wait()
 
 
@@ -614,7 +631,7 @@
         out_shape=tuple(jax.ShapeDtypeStruct(out.shape, out.dtype) for out in outs),
         in_specs=[hbm] * 5,
         out_specs=(hbm,) * 5,
-        scratch_shapes=[dma((5,))],
+        scratch_shapes=[pltpu.VMEM(out.shape, out.dtype) for out in outs] + [dma((2, 14))],
         compiler_params=pltpu.CompilerParams(vmem_limit_bytes=56 * 1024 * 1024),
     )(*outs)
     return (outs[0], outs[1].T) + tuple(outs[2:])

time: 199 us -> 57.4 us (0.29)
  Pallas kernels: 198 us -> 56.6 us
    pallas_call x1, Pallas kernels: 146 us -> 4.42 us  [fused_body(): pl.pallas_call(deliver_kernel, out_shape=tuple((jax.ShapeDtypeStruct(out....]
where the time goes in v7:
time: 57.4 us; the launch traced here: 57.3 us
  Pallas kernels  56.6 us (99%)
  between operations  0.64 us (1%)
    pallas_call x1, Pallas kernels, fused_body(): pl.pallas_call(functools.partial(expert_kernel, tokens, width, share, lan...  52.2 us
    pallas_call x1, Pallas kernels, fused_body(): pl.pallas_call(deliver_kernel, out_shape=tuple((jax.ShapeDtypeStruct(out....  4.42 us

profile of v7, /device:TPU:0, one launch (start us, length us, event | category | flops | bytes accessed | tf_op | source)
XLA Modules:
  0.0 57.3 jit_solution(1909094871537176486)
XLA Ops:
  0.6 52.2 %shard_map.119 = (bf16[16,2048]{1,0:T(8,128)(2,1)}, f32[8,16]{1,0:T(8,128)}, bf16[1,384,2048]{2,1,0:T(8,128)(2,1)}, bf16[1,384,2048]{2,1,0:T(8,128)(2,1)}, bf16[1,384,2048]{2,1,0:T(8,128)(2,1)}) custom-call(bf16[16,2048]{1,0:T(8,128)(2,1)} %grad_hbm.1, bf16[16,2048]{1,0:T(8,128)(2,1)} %codes_hbm.1, bf16[16,16]{1,0:T(8,128)(2,1)} %scales_hbm.1, ...), custom_call_target="tpu_custom_call" | custom-call | tf_op jit(solution)/shard_map/pallas_call | solution.py:585
  52.8 4.4 %shard_map.120 = (bf16[16,2048]{1,0:T(8,128)(2,1)}, f32[8,16]{1,0:T(8,128)}, bf16[1,384,2048]{2,1,0:T(8,128)(2,1)}, bf16[1,384,2048]{2,1,0:T(8,128)(2,1)}, bf16[1,384,2048]{2,1,0:T(8,128)(2,1)}) custom-call(bf16[16,2048]{1,0:T(8,128)(2,1)} %get-tuple-element.15.refs_0_, f32[8,16]{1,0:T(8,128)} %get-tuple-element.16.refs_1_, ...), custom_call_target="tpu_custom_call" | custom-call | tf_op jit(solution)/shard_map/pallas_call | solution.py:629
